TPU v7x, 128 devices: a whole 4x4x4 slice. The times are simulated.
128 devices in a mesh: lat: 8 (over y, core), lon: 8 (over x, z_lo), rep: 2 (over z_hi).
Axes of the slice: x: 4, y: 4, z: 4 (z_hi: 2, z_lo: 2; z = z_hi * 2 + z_lo), core: 2. Of those that a mesh axis runs over, the one named last changes fastest.
Arguments:
- fine_field: bfloat16 [4, 64, 256, 512], P('rep', 'lat', 'lon'), parts along dimension 0, may hold values from -6 to 6
- cotangent: bfloat16 [4, 64, 256, 512], P('rep', 'lat', 'lon'), parts along dimension 0, may hold values from -6 to 6
- land_sea: int32 [64, 256], replicated, may hold values 0 or 1
- shifts: int32 [2], replicated, may hold values from 1 to 7, as said below
- gain_attn: float32 [512], replicated, may hold values from 0.5 to 1.5
- w_qkv: bfloat16 [512, 1536], replicated, may hold values from -0.25 to 0.25
- w_proj: bfloat16 [512, 512], replicated, may hold values from -0.25 to 0.25
- land_bias: float32 [16], replicated, may hold values from -2 to 2
- gain_merge: float32 [2048], replicated, may hold values from 0.5 to 1.5
- w_merge: bfloat16 [2048, 1024], replicated, may hold values from -0.125 to 0.125
- w_expand: bfloat16 [1024, 2048], replicated, may hold values from -0.1875 to 0.1875
Outputs:
- output: bfloat16 [4, 64, 256, 512], P('rep', 'lat', 'lon'), parts along dimension 0
- grad_field: bfloat16 [4, 64, 256, 512], P('rep', 'lat', 'lon'), parts along dimension 0
- grad_qkv: float32 [1024, 1536], P(('rep', 'lat', 'lon')), parts along dimension 0
- grad_proj: float32 [1024, 512], P(('rep', 'lat', 'lon')), parts along dimension 0
- grad_merge: float32 [4096, 1024], P(('rep', 'lat', 'lon')), parts along dimension 0
- grad_expand: float32 [2048, 2048], P(('rep', 'lat', 'lon')), parts along dimension 0
There are 2 independent parts, one for each index of `rep`. A program takes and returns all parts, laid end to end along the dimension named above; an argument that names none is the same for every part. Nothing has to cross between parts.
Inputs may be any that keep to these rules, and one draw needn't show every extreme that they name: `shifts`: one of the two entries is 7, the other lies from 1 to 6.
All inputs are finite; a program needn't handle non-finite values.
Results may differ from a plain program's by a relative error of at most 0.019.
Values may be sent and summed in bfloat16 or wider, within the bound.
A program may use at most 128 MiB of HBM per device.

v0:
```python
from functools import partial

import jax
import jax.numpy as jnp
from jax import lax
from jax.sharding import PartitionSpec as P

WIN = 8


epsilon = 1e-05


def from_behind(value, axis, steps):
    count = lax.axis_size(axis)
    pairs = [(source, (source + steps) % count) for source in range(count)]
    return lax.ppermute(value, axis, pairs)


def layer_norm(values, scales):
    average = jnp.mean(values, axis=-1, keepdims=True)
    centred = values - average
    variance = jnp.mean(centred * centred, axis=-1, keepdims=True)
    return centred * lax.rsqrt(variance + epsilon) * scales


def to_windows(array, window):
    levels, row_count, col_count, features = array.shape
    shaped = array.reshape(
        levels, row_count // window, window, col_count // window, window, features
    )
    return shaped.transpose(1, 3, 0, 2, 4, 5).reshape(-1, levels * window * window, features)


def from_windows(array, levels, row_count, col_count, window):
    features = array.shape[-1]
    shaped = array.reshape(
        row_count // window, col_count // window, levels, window, window, features
    )
    return shaped.transpose(2, 0, 3, 1, 4, 5).reshape(levels, row_count, col_count, features)


def region_of(row_ids, total_rows, shift_lat):
    return (row_ids >= total_rows - WIN).astype(jnp.int32) + (
        row_ids >= total_rows - shift_lat
    ).astype(jnp.int32)


def window_core(queries, window_keys, window_values, land_keys, region, land_bias):
    head_dim = queries.shape[-1]
    scores = jnp.einsum(
        "wqhd,wkhd->whqk", queries.astype(jnp.float32), window_keys.astype(jnp.float32)
    ) * head_dim ** (-0.5)
    scores = scores + land_bias[None, :, None, None] * land_keys[:, None, None, :]
    same_region = region[:, :, None] == region[:, None, :]
    scores = jnp.where(same_region[:, None, :, :], scores, -1000000000.0)
    weights = jax.nn.softmax(scores, axis=-1).astype(jnp.bfloat16)
    mixed_out = jnp.einsum(
        "whqk,wkhd->wqhd", weights.astype(jnp.float32), window_values.astype(jnp.float32)
    )
    return mixed_out.astype(jnp.bfloat16)


def attention_forward(rolled, land_rows, region_rows, gain_attn, w_qkv, w_proj, land_bias):
    levels, row_count, col_count, channels = rolled.shape
    head_count = land_bias.shape[0]
    normed = layer_norm(rolled.astype(jnp.float32), gain_attn).astype(jnp.bfloat16)
    projected = jnp.dot(
        normed.reshape(-1, channels), w_qkv, preferred_element_type=jnp.float32
    ).astype(jnp.bfloat16)
    windows = to_windows(projected.reshape(levels, row_count, col_count, 3 * channels), WIN)
    windows = windows.reshape(
        windows.shape[0], windows.shape[1], 3, head_count, channels // head_count
    )
    land_grid = jnp.broadcast_to(
        land_rows.astype(jnp.float32)[None, :, :, None], (levels, row_count, col_count, 1)
    )
    land_keys = to_windows(land_grid, WIN)[:, :, 0]
    region_grid = jnp.broadcast_to(
        region_rows[None, :, None, None], (levels, row_count, col_count, 1)
    )
    region = to_windows(region_grid, WIN)[:, :, 0]
    mixed_out = window_core(
        windows[:, :, 0], windows[:, :, 1], windows[:, :, 2], land_keys, region, land_bias
    )
    attended = from_windows(
        mixed_out.reshape(mixed_out.shape[0], mixed_out.shape[1], channels),
        levels,
        row_count,
        col_count,
        WIN,
    )
    branch = jnp.dot(
        attended.reshape(-1, channels), w_proj, preferred_element_type=jnp.float32
    ).astype(jnp.bfloat16)
    saved = (rolled, normed, windows, land_keys, region, attended)
    return (branch.reshape(levels, row_count, col_count, channels), saved)


def attention_backward(saved, grad_branch, gain_attn, w_qkv, w_proj, land_bias):
    rolled, normed, windows, land_keys, region, attended = saved
    levels, row_count, col_count, channels = rolled.shape
    grad_flat = grad_branch.reshape(-1, channels)
    grad_proj = jnp.dot(
        attended.reshape(-1, channels).T, grad_flat, preferred_element_type=jnp.float32
    )
    grad_attended = jnp.dot(grad_flat, w_proj.T, preferred_element_type=jnp.float32).astype(
        jnp.bfloat16
    )
    grad_mixed = to_windows(grad_attended.reshape(levels, row_count, col_count, channels), WIN)
    grad_mixed = grad_mixed.reshape(
        windows.shape[0], windows.shape[1], windows.shape[3], windows.shape[4]
    )

    def attend_only(queries, window_keys, window_values):
        return window_core(queries, window_keys, window_values, land_keys, region, land_bias)

    _unused, core_pullback = jax.vjp(
        attend_only, windows[:, :, 0], windows[:, :, 1], windows[:, :, 2]
    )
    grad_q, grad_k, grad_v = core_pullback(grad_mixed)
    grad_windows = jnp.stack((grad_q, grad_k, grad_v), axis=2).reshape(
        windows.shape[0], windows.shape[1], 3 * channels
    )
    grad_projected = from_windows(grad_windows, levels, row_count, col_count, WIN).reshape(
        -1, 3 * channels
    )
    grad_qkv = jnp.dot(
        normed.reshape(-1, channels).T, grad_projected, preferred_element_type=jnp.float32
    )
    grad_normed = jnp.dot(grad_projected, w_qkv.T, preferred_element_type=jnp.float32)
    _unused, norm_pullback = jax.vjp(
        partial(layer_norm, scales=gain_attn), rolled.astype(jnp.float32).reshape(-1, channels)
    )
    grad_rolled = (
        norm_pullback(grad_normed)[0]
        .astype(jnp.bfloat16)
        .reshape(levels, row_count, col_count, channels)
    )
    return (grad_rolled, grad_qkv, grad_proj)


def arrange(grid):
    levels, row_count, col_count, channels = grid.shape
    shaped = grid.reshape(levels, row_count // 2, 2, col_count // 2, 2, channels)
    return shaped.transpose(0, 1, 3, 2, 4, 5).reshape(-1, 4 * channels)


def unarrange(flat, levels, row_count, col_count):
    channels = flat.shape[-1] // 4
    shaped = flat.reshape(levels, row_count // 2, col_count // 2, 2, 2, channels)
    return shaped.transpose(0, 1, 3, 2, 4, 5).reshape(levels, row_count, col_count, channels)


def merge_pass(hidden, cotangent, gain_merge, w_merge, w_expand):
    levels, row_count, col_count, channels = hidden.shape
    merged_f = arrange(hidden).astype(jnp.float32)
    normed = layer_norm(merged_f, gain_merge).astype(jnp.bfloat16)
    coarse = jnp.dot(normed, w_merge, preferred_element_type=jnp.float32)
    activated, gelu_pullback = jax.vjp(jax.nn.gelu, coarse)
    activated = activated.astype(jnp.bfloat16)
    expanded = jnp.dot(activated, w_expand, preferred_element_type=jnp.float32)
    output = (
        hidden.astype(jnp.float32) + unarrange(expanded, levels, row_count, col_count)
    ).astype(jnp.bfloat16)
    grad_up = arrange(cotangent)
    grad_expand = jnp.dot(activated.T, grad_up, preferred_element_type=jnp.float32)
    grad_activated = jnp.dot(grad_up, w_expand.T, preferred_element_type=jnp.float32)
    grad_coarse = gelu_pullback(grad_activated)[0].astype(jnp.bfloat16)
    grad_merge = jnp.dot(normed.T, grad_coarse, preferred_element_type=jnp.float32)
    grad_normed = jnp.dot(grad_coarse, w_merge.T, preferred_element_type=jnp.float32)
    _unused, norm_pullback = jax.vjp(partial(layer_norm, scales=gain_merge), merged_f)
    grad_hidden = cotangent.astype(jnp.float32) + unarrange(
        norm_pullback(grad_normed)[0], levels, row_count, col_count
    )
    return (output, grad_hidden, grad_merge, grad_expand)


def roll_minus(grid, shift_lat, shift_lon):
    rim_width = WIN - 1
    rim_rows = lax.slice_in_dim(grid, 0, rim_width, axis=1)
    arrived = from_behind(rim_rows, "lat", -1)
    joined = jnp.concatenate((grid, arrived), axis=1)
    grid = lax.dynamic_slice_in_dim(joined, shift_lat, grid.shape[1], axis=1)
    rim_cols = lax.slice_in_dim(grid, 0, rim_width, axis=2)
    arrived = from_behind(rim_cols, "lon", -1)
    joined = jnp.concatenate((grid, arrived), axis=2)
    return lax.dynamic_slice_in_dim(joined, shift_lon, grid.shape[2], axis=2)


def roll_plus(grid, shift_lat, shift_lon):
    rim_width = WIN - 1
    row_total = grid.shape[1]
    rim_rows = lax.slice_in_dim(grid, row_total - rim_width, row_total, axis=1)
    arrived = from_behind(rim_rows, "lat", 1)
    joined = jnp.concatenate((arrived, grid), axis=1)
    grid = lax.dynamic_slice_in_dim(joined, rim_width - shift_lat, row_total, axis=1)
    col_total = grid.shape[2]
    rim_cols = lax.slice_in_dim(grid, col_total - rim_width, col_total, axis=2)
    arrived = from_behind(rim_cols, "lon", 1)
    joined = jnp.concatenate((arrived, grid), axis=2)
    return lax.dynamic_slice_in_dim(joined, rim_width - shift_lon, col_total, axis=2)


def on_device(
    fine_field,
    cotangent,
    land_sea,
    shifts,
    gain_attn,
    w_qkv,
    w_proj,
    land_bias,
    gain_merge,
    w_merge,
    w_expand,
):
    levels, row_count, col_count, channels = fine_field.shape
    shift_lat = shifts[0]
    shift_lon = shifts[1]
    lat_index = lax.axis_index("lat")
    lon_index = lax.axis_index("lon")
    land_all = jnp.roll(land_sea, (-shift_lat, -shift_lon), axis=(0, 1))
    land_rolled = lax.dynamic_slice(
        land_all, (lat_index * row_count, lon_index * col_count), (row_count, col_count)
    )
    row_ids = lat_index * row_count + jnp.arange(row_count, dtype=jnp.int32)
    region_rows = region_of(row_ids, land_sea.shape[0], shift_lat)
    rolled = roll_minus(fine_field, shift_lat, shift_lon)
    branch, saved = attention_forward(
        rolled, land_rolled, region_rows, gain_attn, w_qkv, w_proj, land_bias
    )
    rolled_back = roll_plus(branch, shift_lat, shift_lon)
    hidden = (fine_field.astype(jnp.float32) + rolled_back.astype(jnp.float32)).astype(jnp.bfloat16)
    output, grad_hidden, grad_merge, grad_expand = merge_pass(
        hidden, cotangent, gain_merge, w_merge, w_expand
    )
    grad_branch = roll_minus(grad_hidden.astype(jnp.bfloat16), shift_lat, shift_lon)
    grad_rolled, grad_qkv, grad_proj = attention_backward(
        saved, grad_branch, gain_attn, w_qkv, w_proj, land_bias
    )
    grad_back = roll_plus(grad_rolled, shift_lat, shift_lon)
    grad_field = (grad_hidden + grad_back.astype(jnp.float32)).astype(jnp.bfloat16)
    reduced = (
        lax.psum_scatter(grad_qkv, ("lat", "lon"), scatter_dimension=0, tiled=True),
        lax.psum_scatter(grad_proj, ("lat", "lon"), scatter_dimension=0, tiled=True),
        lax.psum_scatter(grad_merge, ("lat", "lon"), scatter_dimension=0, tiled=True),
        lax.psum_scatter(grad_expand, ("lat", "lon"), scatter_dimension=0, tiled=True),
    )
    return (output, grad_field, reduced[0], reduced[1], reduced[2], reduced[3])


def solution(mesh):
    return jax.shard_map(
        on_device,
        mesh=mesh,
        in_specs=(
            P("rep", "lat", "lon", None),
            P("rep", "lat", "lon", None),
            P(),
            P(),
            P(),
            P(),
            P(),
            P(),
            P(),
            P(),
            P(),
        ),
        out_specs=(
            P("rep", "lat", "lon", None),
            P("rep", "lat", "lon", None),
            P(("rep", "lat", "lon"), None),
            P(("rep", "lat", "lon"), None),
            P(("rep", "lat", "lon"), None),
            P(("rep", "lat", "lon"), None),
        ),
        check_vma=False,
    )
```

profile of v0, /device:TPU:1, one launch (start us, length us, event | category | flops | bytes accessed | tf_op | source)
XLA Modules:
  0.0 1318.5 jit_solution(3902180994896360070)
XLA Ops:
  20.8 4.0 collective-permute-start.1
  31.5 8.0 reshape_reshape.26
  39.5 6.0 fusion.57
  45.5 2.8 copy.50
  48.3 3.0 copy.51
  51.3 3.6 copy.52
  66.4 3.4 reshape_reshape.27
  73.0 2.9 collective-permute-start.2
  85.3 4.5 fusion.61
  100.3 4.3 fusion.27
  107.8 3.1 reshape.202
  110.9 2.7 copy.37
  113.7 2.9 reshape.203
  118.2 4.3 collective-permute-start.4
  122.5 5.1 collective-permute-done.4
  137.4 3.6 reshape_reshape.30
  141.0 3.4 copy.39
  144.4 2.9 fusion.13
  147.4 3.7 fusion.6
  155.0 7.5 copy.44
  162.5 9.3 reshape_reshape.31
  174.5 3.7 fusion.62
  178.3 4.6 fusion.51
  184.2 4.5 fusion.47
  197.7 3.2 reshape.198
  200.9 2.8 copy.35
  203.7 2.9 reshape.199
  210.2 5.0 collective-permute-done.7
  216.4 198.4 %reduce-scatter.7.cloned.1.call-done = f32[8,512]{1,0:T(8,128)} async-done(((f32[512,512]{1,0:T(8,128)}), f32[8,512]{1,0:T(8,128)}) %reduce-scatter.7.cloned.1.call-update) | async-done | bytes 16400 | tf_op jit(solution)/shard_map/reduce_scatter | solution.py:246
  414.8 288.9 %reduce-scatter.5.cloned.1.call-done = f32[8,1536]{1,0:T(8,128)} async-done(((f32[512,1536]{1,0:T(8,128)}), f32[8,1536]{1,0:T(8,128)}) %reduce-scatter.5.cloned.1.call-update) | async-done | bytes 49168 | tf_op jit(solution)/shard_map/reduce_scatter | solution.py:245
  703.7 303.3 %reduce-scatter.9.cloned.1.call-done = f32[32,1024]{1,0:T(8,128)} async-done(((f32[2048,1024]{1,0:T(8,128)}), f32[32,1024]{1,0:T(8,128)}) %reduce-scatter.9.cloned.1.call-update) | async-done | bytes 131088 | tf_op jit(solution)/shard_map/reduce_scatter | solution.py:247
  1007.0 304.5 %reduce-scatter.11.cloned.1.call-done = f32[16,2048]{1,0:T(8,128)} async-done(((f32[1024,2048]{1,0:T(8,128)}), f32[16,2048]{1,0:T(8,128)}) %reduce-scatter.11.cloned.1.call-update) | async-done | bytes 131088 | tf_op jit(solution)/shard_map/reduce_scatter | solution.py:248
  (165 shorter events, 81.1 us)
Async XLA Ops:
  7.2 22.1 %copy-start = (bf16[512,1536]{1,0:T(8,128)(2,1)S(1)}, bf16[512,1536]{1,0:T(8,128)(2,1)}, u32[]{:S(2)}) copy-start(bf16[512,1536]{1,0:T(8,128)(2,1)} %param.16) | copy-start | bytes 4718596
  7.2 21.0 %copy-start.32 = (f32[512]{0:T(512)S(1)}, f32[512]{0:T(512)}, u32[]{:S(2)}) copy-start(f32[512]{0:T(512)} %param.15) | copy-start | bytes 6148
  7.2 407.6 %reduce-scatter.7.cloned.1.call-start = ((), (), s32[]{:S(2)}) async-start(), calls=%async_computation.5 | async-start | bytes 1064960 | tf_op jit(solution)/shard_map/reduce_scatter | solution.py:246
  8.4 11.4 collective-permute-start
  20.8 5.9 collective-permute-start.1
  48.3 13.5 %copy-start.8 = (bf16[4,128,1,16,32]{1,4,3,0,2:T(8,128)(2,1)}, bf16[4,128,1,16,32]{1,4,3,0,2:T(8,128)(2,1)S(1)}, u32[]{:S(2)}) copy-start(bf16[4,128,1,16,32]{1,4,3,0,2:T(8,128)(2,1)S(1)} %copy.50) | copy-start | bytes 1572868
  51.3 8.0 copy-start.22
  63.8 13.4 %copy-start.12 = (bf16[2,8,32,512]{3,2,1,0:T(8,128)(2,1)S(1)}, bf16[2,8,32,512]{3,2,1,0:T(8,128)(2,1)}, u32[]{:S(2)}) copy-start(bf16[2,8,32,512]{3,2,1,0:T(8,128)(2,1)} %param.12) | copy-start | bytes 1572868
  72.1 6.2 copy-start.17
  73.0 9.0 collective-permute-start.2
  80.5 10.7 copy-start.16
  82.0 9.2 copy-start.14
  84.2 7.0 collective-permute-start.3
  93.5 6.8 copy-start.26
  95.8 10.4 copy-start.28
  100.3 4.3 copy-start.19
  100.3 6.0 copy-start.30
  116.6 16.6 %copy-start.10 = (bf16[2,1,8,4,8,512]{5,4,3,2,0,1:T(8,128)(2,1)S(1)}, bf16[2,1,8,4,8,512]{5,4,3,2,0,1:T(8,128)(2,1)}, u32[]{:S(2)}) copy-start(bf16[2,1,8,4,8,512]{5,4,3,2,0,1:T(8,128)(2,1)} %copy-done.9) | copy-start | bytes 1572868
  118.2 9.4 collective-permute-start.4
  127.8 4.2 collective-permute-start.5
  137.2 566.6 %reduce-scatter.5.cloned.1.call-start = ((), (), s32[]{:S(2)}) async-start(), calls=%async_computation.4 | async-start | bytes 3194880 | tf_op jit(solution)/shard_map/reduce_scatter | solution.py:245
  147.4 3.9 copy-start.24
  174.5 3.8 copy-start.29
  174.5 3.8 copy-start.31
  178.3 828.8 %reduce-scatter.9.cloned.1.call-start = ((), (), s32[]{:S(2)}) async-start(), calls=%async_computation.6 | async-start | bytes 8519680 | tf_op jit(solution)/shard_map/reduce_scatter | solution.py:247
  183.0 1128.5 %reduce-scatter.11.cloned.1.call-start = ((), (), s32[]{:S(2)}) async-start(), calls=%async_computation.7 | async-start | bytes 8519680 | tf_op jit(solution)/shard_map/reduce_scatter | solution.py:248
  189.5 6.4 copy-start.4
  194.4 12.3 collective-permute-start.6
  197.7 10.3 copy-start.5
  200.9 14.3 %copy-start.13 = (bf16[2,8,32,512]{3,2,1,0:T(8,128)(2,1)S(1)}, bf16[2,8,32,512]{3,2,1,0:T(8,128)(2,1)}, u32[]{:S(2)}) copy-start(bf16[2,8,32,512]{3,2,1,0:T(8,128)(2,1)} %param.12) | copy-start | bytes 1572868
  206.6 8.6 copy-start.6
  208.0 7.3 collective-permute-start.7
  (14 other events, 17.2 us)
Sparse Core Ops, SparseCore 0:
  137.3 277.4 reduce-scatter.6
  417.8 285.8 reduce-scatter.4
  706.7 300.2 reduce-scatter.8
  1009.8 301.6 reduce-scatter.10
where the time goes:
time: 1340 us; the launch traced here: 1320 us
  waiting for transfers between devices  1110 us (83%)
  local copies, waits for them, and re-layouts  99.6 us (7%)
  matrix products  44.8 us (3%)
  between operations  24.6 us (2%)
  other arithmetic  22.8 us (2%)
  starting transfers between devices  18.3 us (1%)
    reduce_scatter x1, waiting for transfers between devices, on_device(): lax.psum_scatter(grad_expand, ('lat', 'lon'), scatter_dimension=0, tiled=...  304 us
    reduce_scatter x1, waiting for transfers between devices, on_device(): lax.psum_scatter(grad_merge, ('lat', 'lon'), scatter_dimension=0, tiled=T...  303 us
    reduce_scatter x1, waiting for transfers between devices, on_device(): lax.psum_scatter(grad_qkv, ('lat', 'lon'), scatter_dimension=0, tiled=True)  289 us
    reduce_scatter x1, waiting for transfers between devices, on_device(): lax.psum_scatter(grad_proj, ('lat', 'lon'), scatter_dimension=0, tiled=True)  198 us
  transfers between devices with their start and end apart: 12, of which 8 were waited for; matrix products, arithmetic and copies ran while one was open for 6% of the time, Pallas kernels for 0%

commit v1 on v0

--- a/solution.py
+++ b/solution.py
@@ -3,6 +3,8 @@
 import jax
 import jax.numpy as jnp
 from jax import lax
+from jax.experimental import pallas as pl
+from jax.experimental.pallas import tpu as pltpu
 from jax.sharding import PartitionSpec as P
 
 WIN = 8
@@ -200,6 +202,299 @@
     arrived = from_behind(rim_cols, "lon", 1)
     joined = jnp.concatenate((arrived, grid), axis=2)
     return lax.dynamic_slice_in_dim(joined, rim_width - shift_lon, col_total, axis=2)
+
+
+MESH = pl.DeviceIdType.MESH
+
+
+class Ring:
+    def __init__(self, place, right, left, block, store, bufs, send_sems, recv_sems, lead, half):
+        self.place, self.right, self.left = place, right, left
+        self.block, self.store = block, store
+        self.bufs, self.outs = bufs[0], bufs[1]
+        self.send_sems, self.recv_sems = send_sems, recv_sems
+        self.lead, self.half = lead, half
+        self.copies = {}
+
+    def part(self, k, which):
+        return self.block(k).at[:, :, pl.ds(which * self.half, self.half)]
+
+    def copy(self, slot, source, target):
+        made = pltpu.make_async_remote_copy(
+            src_ref=source,
+            dst_ref=self.bufs.at[slot],
+            send_sem=self.send_sems.at[slot],
+            recv_sem=self.recv_sems.at[slot],
+            device_id=target,
+            device_id_type=MESH,
+        )
+        made.start()
+        self.copies[slot] = made
+
+    def begin(self):
+        ahead = lax.rem(self.place + 1, 4)
+        across = lax.rem(self.place + 2, 4)
+        behind = lax.rem(self.place + 3, 4)
+        self.copy(0, self.part(across, 0), self.right)
+        self.copy(3, self.part(across, 1), self.left)
+        self.copy(1, self.part(ahead, 1), self.right)
+        self.copy(4, self.part(behind, 0), self.left)
+
+    def middle(self):
+        ahead = lax.rem(self.place + 1, 4)
+        behind = lax.rem(self.place + 3, 4)
+        for slot, which, k, out, target in ((0, 0, ahead, 0, self.right), (3, 1, behind, 1, self.left)):
+            self.copies[slot].wait_recv()
+
+            def add(i, carry, slot=slot, which=which, k=k, out=out):
+                mine = self.block(k)[i, :, pl.ds(which * self.half, self.half)]
+                total = mine.astype(jnp.float32) + self.bufs[slot, i].astype(jnp.float32)
+                self.outs[out, i] = total.astype(jnp.bfloat16)
+                return carry
+
+            lax.fori_loop(0, self.lead, add, 0)
+            self.copy(2 if out == 0 else 5, self.outs.at[out], target)
+
+    def finish(self):
+        for slot in (1, 2, 4, 5):
+            self.copies[slot].wait_recv()
+
+        def add(i, carry):
+            for which, first, second in ((0, 2, 4), (1, 5, 1)):
+                mine = self.block(self.place)[i, :, pl.ds(which * self.half, self.half)]
+                total = (
+                    mine.astype(jnp.float32)
+                    + self.bufs[first, i].astype(jnp.float32)
+                    + self.bufs[second, i].astype(jnp.float32)
+                )
+                self.store(i, which, total)
+            return carry
+
+        lax.fori_loop(0, self.lead, add, 0)
+
+    def drain(self):
+        for slot in range(6):
+            self.copies[slot].wait_send()
+
+
+class Stream:
+    def __init__(self, where, source, first_axis, scratch, store):
+        red, buf1, out1, buf2, out2, fin, zsend, zrecv, ssem, rsem = scratch
+        self.where, self.scratch, self.store = where, scratch, store
+        self.rows, self.width = source.shape[2], source.shape[3]
+        half = self.width // 2
+        axes = {
+            "y": (where["y"], where["up"], where["down"], lambda k: source.at[k]),
+            "x": (where["x"], where["east"], where["west"], lambda k: source.at[:, k]),
+        }
+        second_axis = "x" if first_axis == "y" else "y"
+
+        def store_red(i, which, total):
+            red[i, 0, :, pl.ds(which * half, half)] = total.astype(jnp.bfloat16)
+
+        def store_fin(i, which, total):
+            deep = self.rows // 2
+            for z in range(2):
+                fin[z, :, pl.ds(which * half, half)] = total[z * deep : (z + 1) * deep]
+
+        place, right, left, block = axes[first_axis]
+        self.ring1 = Ring(
+            place, right, left, block, store_red, (buf1, out1), ssem.at[pl.ds(0, 6)], rsem.at[pl.ds(0, 6)], 4, half
+        )
+        place, right, left, _unused = axes[second_axis]
+        self.ring2 = Ring(
+            place,
+            right,
+            left,
+            lambda k: red.at[k],
+            store_fin,
+            (buf2, out2),
+            ssem.at[pl.ds(6, 6)],
+            rsem.at[pl.ds(6, 6)],
+            1,
+            half,
+        )
+
+    def z_begin(self):
+        _r, _a, _b, _c, _d, fin, zsend, zrecv, ssem, rsem = self.scratch
+        zsend[...] = fin[1 - self.where["z"]].astype(zsend.dtype)
+        self.z_copy = pltpu.make_async_remote_copy(
+            src_ref=zsend,
+            dst_ref=zrecv,
+            send_sem=ssem.at[12],
+            recv_sem=rsem.at[12],
+            device_id=self.where["beside"],
+            device_id_type=MESH,
+        )
+        self.z_copy.start()
+
+    def z_finish(self):
+        fin, zrecv = self.scratch[5], self.scratch[7]
+        self.z_copy.wait_recv()
+        self.store(fin[self.where["z"]] + zrecv[...].astype(jnp.float32))
+
+    def drain(self):
+        self.ring1.drain()
+        self.ring2.drain()
+        self.z_copy.wait_send()
+
+
+def stream_scratch(rows, width, z_type):
+    half = width // 2
+    deep = rows // 2
+    return [
+        pltpu.VMEM((4, 1, rows, width), jnp.bfloat16),
+        pltpu.VMEM((6, 4, rows, half), jnp.bfloat16),
+        pltpu.VMEM((2, 4, rows, half), jnp.bfloat16),
+        pltpu.VMEM((6, 1, rows, half), jnp.bfloat16),
+        pltpu.VMEM((2, 1, rows, half), jnp.bfloat16),
+        pltpu.VMEM((2, deep, width), jnp.float32),
+        pltpu.VMEM((deep, width), z_type),
+        pltpu.VMEM((deep, width), z_type),
+        pltpu.SemaphoreType.DMA((13,)),
+        pltpu.SemaphoreType.DMA((13,)),
+    ]
+
+
+def places():
+    lat, lon = lax.axis_index("lat"), lax.axis_index("lon")
+    core, z = lax.rem(lat, 2), lax.rem(lon, 2)
+    return {
+        "lat": lat,
+        "lon": lon,
+        "y": lat // 2,
+        "x": lon // 2,
+        "core": core,
+        "z": z,
+        "up": {"lat": lax.rem(lat + 2, 8)},
+        "down": {"lat": lax.rem(lat + 6, 8)},
+        "east": {"lon": lax.rem(lon + 2, 8)},
+        "west": {"lon": lax.rem(lon + 6, 8)},
+        "beside": {"lon": lon + 1 - 2 * z},
+        "sibling": {"lat": lat + 1 - 2 * core},
+    }
+
+
+def reduce_kernel(at_ref, ex_ref, mg_ref, qkv_out, proj_out, mg_out, ex_out, *scratch):
+    where = places()
+    core = where["core"]
+    acc_at1, acc_at2, acc_ex, acc_mg, got_at, got_ex, got_mg, csem, crsem = scratch[:9]
+    barrier = pltpu.get_barrier_semaphore()
+    for name in ("up", "down", "east", "west", "beside", "sibling"):
+        pl.semaphore_signal(barrier, inc=1, device_id=where[name], device_id_type=MESH)
+    pl.semaphore_wait(barrier, 6)
+
+    firsts = []
+    for n, (source, target) in enumerate(((ex_ref, got_ex), (mg_ref, got_mg), (at_ref, got_at))):
+        made = pltpu.make_async_remote_copy(
+            src_ref=source.at[:, 1 - core],
+            dst_ref=target,
+            send_sem=csem.at[n],
+            recv_sem=crsem.at[n],
+            device_id=where["sibling"],
+            device_id_type=MESH,
+        )
+        made.start()
+        firsts.append(made)
+
+    def store_at1(value):
+        qkv_out[:, 0:1024] = value
+
+    def store_at2(value):
+        qkv_out[:, 1024:1536] = value[:, :512]
+        proj_out[...] = value[:, 512:]
+
+    def store_ex(value):
+        ex_out[...] = value
+
+    def store_mg(value):
+        mg_out[...] = value
+
+    streams = [
+        Stream(where, acc_ex, "y", scratch[9:19], store_ex),
+        Stream(where, acc_mg, "x", scratch[19:29], store_mg),
+        Stream(where, acc_at1, "y", scratch[29:39], store_at1),
+        Stream(where, acc_at2, "x", scratch[39:49], store_at2),
+    ]
+
+    def sum_into(source, got, targets):
+        def add(n, carry):
+            y, x = n // 4, lax.rem(n, 4)
+            total = source[y, core, x].astype(jnp.float32) + got[y, x].astype(jnp.float32)
+            total = total.astype(jnp.bfloat16)
+            start = 0
+            for target in targets:
+                width = target.shape[3]
+                target[y, x] = total[:, start : start + width]
+                start += width
+            return carry
+
+        lax.fori_loop(0, 16, add, 0)
+
+    firsts[0].wait_recv()
+    sum_into(ex_ref, got_ex, [acc_ex])
+    streams[0].ring1.begin()
+    firsts[1].wait_recv()
+    sum_into(mg_ref, got_mg, [acc_mg])
+    streams[1].ring1.begin()
+    firsts[2].wait_recv()
+    sum_into(at_ref, got_at, [acc_at1, acc_at2])
+    streams[2].ring1.begin()
+    streams[3].ring1.begin()
+    for stream in streams:
+        stream.ring1.middle()
+    for stream in streams:
+        stream.ring1.finish()
+        stream.ring2.begin()
+    for stream in streams:
+        stream.ring2.middle()
+    for stream in streams:
+        stream.ring2.finish()
+        stream.z_begin()
+    for stream in streams:
+        stream.z_finish()
+    for made in firsts:
+        made.wait_send()
+    for stream in streams:
+        stream.drain()
+
+
+def reduce_all(grad_qkv, grad_proj, grad_merge, grad_expand):
+    at = jnp.concatenate((grad_qkv, grad_proj), axis=1).astype(jnp.bfloat16).reshape(4, 2, 4, 16, 2048)
+    ex = grad_expand.astype(jnp.bfloat16).reshape(4, 2, 4, 32, 2048)
+    mg = grad_merge.astype(jnp.bfloat16).reshape(4, 2, 4, 64, 1024)
+    vmem = pl.BlockSpec(memory_space=pltpu.VMEM)
+    bf16 = jnp.bfloat16
+    return pl.pallas_call(
+        reduce_kernel,
+        out_shape=(
+            jax.ShapeDtypeStruct((8, 1536), jnp.float32),
+            jax.ShapeDtypeStruct((8, 512), jnp.float32),
+            jax.ShapeDtypeStruct((32, 1024), jnp.float32),
+            jax.ShapeDtypeStruct((16, 2048), jnp.float32),
+        ),
+        in_specs=[vmem] * 3,
+        out_specs=(vmem,) * 4,
+        scratch_shapes=[
+            pltpu.VMEM((4, 4, 16, 1024), bf16),
+            pltpu.VMEM((4, 4, 16, 1024), bf16),
+            pltpu.VMEM((4, 4, 32, 2048), bf16),
+            pltpu.VMEM((4, 4, 64, 1024), bf16),
+            pltpu.VMEM((4, 4, 16, 2048), bf16),
+            pltpu.VMEM((4, 4, 32, 2048), bf16),
+            pltpu.VMEM((4, 4, 64, 1024), bf16),
+            pltpu.SemaphoreType.DMA((3,)),
+            pltpu.SemaphoreType.DMA((3,)),
+        ]
+        + stream_scratch(32, 2048, bf16)
+        + stream_scratch(64, 1024, bf16)
+        + stream_scratch(16, 1024, jnp.float32)
+        + stream_scratch(16, 1024, jnp.float32),
+        compiler_params=pltpu.CompilerParams(
+            collective_id=0, has_side_effects=True, vmem_limit_bytes=56 * 2**20
+        ),
+        name="reduce_gradients",
+    )(at, ex, mg)
 
 
 def on_device(
@@ -241,12 +536,7 @@
     )
     grad_back = roll_plus(grad_rolled, shift_lat, shift_lon)
     grad_field = (grad_hidden + grad_back.astype(jnp.float32)).astype(jnp.bfloat16)
-    reduced = (
-        lax.psum_scatter(grad_qkv, ("lat", "lon"), scatter_dimension=0, tiled=True),
-        lax.psum_scatter(grad_proj, ("lat", "lon"), scatter_dimension=0, tiled=True),
-        lax.psum_scatter(grad_merge, ("lat", "lon"), scatter_dimension=0, tiled=True),
-        lax.psum_scatter(grad_expand, ("lat", "lon"), scatter_dimension=0, tiled=True),
-    )
+    reduced = reduce_all(grad_qkv, grad_proj, grad_merge, grad_expand)
     return (output, grad_field, reduced[0], reduced[1], reduced[2], reduced[3])
 
 

time: 1340 us -> 262 us (0.20); the launches traced: 1320 us -> 258 us
  waiting for transfers between devices: 1110 us -> 13.6 us
  Pallas kernels: 0 us -> 54 us
    reduce_scatter x4 -> x0, waiting for transfers between devices: 1100 us -> none  [the longest x1 304 us: on_device(): lax.psum_scatter(grad_expand, ('lat', 'lon'), scatter_dimension=0, tiled=...]
    pallas_call x0 -> x1, Pallas kernels: none -> 54 us  [reduce_all(): pl.pallas_call(reduce_kernel, out_shape=(jax.ShapeDtypeStruct((8, 1536),...]
  transfers between devices with their start and end apart: 12 -> 8, of which waited for: 8 -> 4; matrix products, arithmetic and copies ran while one was open for 6% -> 15% of each run, Pallas kernels for 0% -> 21%
where the time goes in v1:
time: 262 us; the launch traced here: 258 us
  local copies, waits for them, and re-layouts  105 us (40%)
  Pallas kernels  54 us (21%)
  matrix products  37.1 us (14%)
  other arithmetic  22.3 us (9%)
  starting transfers between devices  14.2 us (5%)
  waiting for transfers between devices  13.6 us (5%)
  between operations  11.3 us (4%)
    pallas_call x1, Pallas kernels, reduce_all(): pl.pallas_call(reduce_kernel, out_shape=(jax.ShapeDtypeStruct((8, 1536),...  54 us
    unnamed x75, local copies, waits for them, and re-layouts  22.7 us
    ppermute x8, starting transfers between devices, from_behind(): return lax.ppermute(value, axis, pairs)  14.2 us
    ppermute x8, waiting for transfers between devices, from_behind(): return lax.ppermute(value, axis, pairs)  13.6 us
    another operation x2, local copies, waits for them, and re-layouts, from_windows(): array.reshape(row_count // window, col_count // window, levels, window, w...  13.4 us
    another operation x1, local copies, waits for them, and re-layouts, attention_forward(): windows.reshape(windows.shape[0], windows.shape[1], 3, head_count, channe...  8.47 us
    another operation x1, local copies, waits for them, and re-layouts, attention_backward(): jnp.stack((grad_q, grad_k, grad_v), axis=2)  7.44 us
    dot_general x3, matrix products, window_core(): jnp.einsum('whqk,wkhd->wqhd', weights.astype(jnp.float32), window_values....  6.78 us
  transfers between devices with their start and end apart: 8, of which 4 were waited for; matrix products, arithmetic and copies ran while one was open for 15% of the time, Pallas kernels for 21%

profile of v1, /device:TPU:1, one launch (start us, length us, event | category | flops | bytes accessed | tf_op | source)
XLA Modules:
  0.0 257.7 jit_solution(6655003236058360022)
XLA Ops:
  14.4 4.0 %collective-permute-start.1 = (bf16[2,8,7,512]{3,2,1,0:T(8,128)(2,1)S(1)}, bf16[2,8,7,512]{3,2,1,0:T(8,128)(2,1)S(1)}, u32[]{:S(2)}, u32[]{:S(2)}) collective-permute-start(bf16[2,8,7,512]{3,2,1,0:T(8,128)(2,1)S(1)} %slice.55), channel_id=1, source_target_pairs={{0,14},{2,0},{4,2},{6,4},{8,6},{10,8},{12,10},{14,12},{1,15},{3,1}... | collective-permute-start | bytes 344072 | tf_op jit(solution)/shard_map/ppermute | solution.py:19
  24.5 8.5 %reshape_reshape.26 = bf16[4,128,3,16,32]{4,3,2,1,0:T(8,128)(2,1)} reshape(bf16[1,4,2,8,8,1536]{5,4,3,2,1,0:T(8,128)(2,1)} %bitcast.130) | data formatting | bytes 3145728 | tf_op jit(solution)/shard_map/reshape;reshape | solution.py:74
  33.0 6.0 %fusion.55 = (bf16[4,128,1,16,32]{4,3,2,1,0:T(8,128)(2,1)}, bf16[4,128,1,16,32]{4,3,2,1,0:T(8,128)(2,1)}, bf16[4,128,1,16,32]{4,3,2,1,0:T(8,128)(2,1)}) fusion(bf16[4,128,3,16,32]{4,3,2,1,0:T(8,128)(2,1)} %reshape_reshape.26), kind=kLoop, calls=%fused_computation.131 | loop fusion | bytes 3145728 | tf_op jit(solution)/shard_map/slice | solution.py:86
  39.0 2.8 %copy.79 = bf16[4,128,1,16,32]{1,4,3,0,2:T(8,128)(2,1)S(1)} copy(bf16[4,128,1,16,32]{4,3,2,1,0:T(8,128)(2,1)} %get-tuple-element.22) | data formatting | bytes 1048576
  41.7 3.6 %copy.78 = bf16[4,128,1,16,32]{1,4,3,0,2:T(8,128)(2,1)} copy(bf16[4,128,1,16,32]{4,3,2,1,0:T(8,128)(2,1)} %get-tuple-element.21) | data formatting | bytes 1048576
  45.3 2.8 %copy.77 = bf16[4,128,1,16,32]{1,4,3,0,2:T(8,128)(2,1)S(1)} copy(bf16[4,128,1,16,32]{4,3,2,1,0:T(8,128)(2,1)} %get-tuple-element.20) | data formatting | bytes 1048576
  50.1 2.6 fusion.58
  57.2 2.5 copy.55
  59.8 4.1 %reshape_reshape.27 = bf16[1,4,2,8,8,512]{5,4,3,2,1,0:T(8,128)(2,1)} reshape(bf16[4,128,16,32]{3,2,1,0:T(8,128)(2,1)} %copy.55) | data formatting | bytes 1048576 | tf_op jit(solution)/shard_map/reshape;reshape | solution.py:39
  68.0 3.0 %collective-permute-start.2 = (bf16[2,7,32,512]{3,2,1,0:T(8,128)(2,1)}, bf16[2,7,32,512]{3,2,1,0:T(8,128)(2,1)}, u32[]{:S(2)}, u32[]{:S(2)}) collective-permute-start(bf16[2,7,32,512]{3,2,1,0:T(8,128)(2,1)} %slice.59), channel_id=1, source_target_pairs={{0,16},{16,32},{32,48},{48,64},{64,80},{80,96},{96,112},{112,0},{1... | collective-permute-start | bytes 1376264 | tf_op jit(solution)/shard_map/ppermute | solution.py:19
  74.6 2.2 copy.91
  78.3 4.7 %fusion.59 = f32[128,1024]{1,0:T(8,128)} fusion(bf16[128,2048]{1,0:T(8,128)(2,1)S(1)} %reshape.212, bf16[1024,2048]{1,0:T(8,128)(2,1)} %param.21), kind=kOutput, calls=%fused_computation.135 | convolution fusion | flops 536870912 | bytes 5242880 | tf_op jit(solution)/shard_map/dot_general | solution.py:170
  88.6 7.0 %collective-permute-done.3 = bf16[2,8,7,512]{3,2,1,0:T(8,128)(2,1)S(1)} collective-permute-done((bf16[2,8,7,512]{3,2,1,0:T(8,128)(2,1)S(1)}, bf16[2,8,7,512]{3,2,1,0:T(8,128)(2,1)S(1)}, u32[]{:S(2)}, u32[]{:S(2)}) %collective-permute-start.3) | collective-permute-done | bytes 114720 | tf_op jit(solution)/shard_map/ppermute | solution.py:19
  95.6 2.3 fusion.32
  102.9 2.1 reshape.220
  105.7 3.6 %fusion.27 = (bf16[128,1024]{1,0:T(8,128)(2,1)S(1)}, f32[128,1024]{1,0:T(8,128)S(1)}) fusion(f32[128,1024]{1,0:T(8,128)} %fusion.59, bf16[2048,1024]{1,0:T(8,128)(2,1)} %param.20, f32[128,2048]{1,0:T(8,128)S(1)} %reshape.220, f32[2048]{0:T(1024)S(1)} %copy-done.27, f32[128]{0:T(128)S(1)} %rsqrt.30, f32[128]{0:T(128)} %div.75), kind=kOutput, calls=%fused_computation.84 | convolution fusion | flops 540540928 | bytes 6562816 | tf_op jit(solution)/shard_map/dot_general | solution.py:161
  115.3 3.1 %reshape.213 = f32[2,4,16,2,2,512]{5,4,3,2,1,0:T(2,128)} reshape(f32[128,2048]{1,0:T(8,128)} %broadcast_add_fusion) | data formatting | bytes 2097152 | tf_op jit(solution)/shard_map/reshape | solution.py:153
  118.4 2.7 %copy.60 = f32[2,4,2,16,2,512]{5,4,3,2,1,0:T(2,128)} copy(f32[2,4,2,16,2,512]{5,4,2,3,1,0:T(2,128)} %bitcast.141) | data formatting | bytes 2097152 | tf_op jit(solution)/shard_map/transpose | solution.py:154
  121.1 2.9 %reshape.214 = f32[2,8,32,512]{3,2,1,0:T(8,128)} reshape(f32[2,4,2,16,2,512]{5,4,3,2,1,0:T(2,128)} %copy.60) | data formatting | bytes 2097152 | tf_op jit(solution)/shard_map/reshape | solution.py:154
  128.0 4.6 %convolution_convert_fusion.1 = bf16[1024,2048]{1,0:T(8,128)(2,1)} fusion(bf16[128,2048]{1,0:T(8,128)(2,1)} %copy-done.9, f32[128,1024]{1,0:T(8,128)} %copy-done.19), kind=kOutput, calls=%fused_computation.13 | convolution fusion | flops 540147712 | bytes 5242880 | tf_op jit(solution)/shard_map/dot_general | solution.py:169
  132.6 3.1 %reshape.209 = f32[2,4,16,2,2,512]{5,4,3,2,1,0:T(2,128)} reshape(f32[128,2048]{1,0:T(8,128)} %fusion.47) | data formatting | bytes 2097152 | tf_op jit(solution)/shard_map/reshape | solution.py:153
  135.7 2.7 %copy.58 = f32[2,4,2,16,2,512]{5,4,3,2,1,0:T(2,128)} copy(f32[2,4,2,16,2,512]{5,4,2,3,1,0:T(2,128)} %bitcast.142) | data formatting | bytes 2097152 | tf_op jit(solution)/shard_map/transpose | solution.py:154
  138.4 2.9 %reshape.210 = f32[2,8,32,512]{3,2,1,0:T(8,128)} reshape(f32[2,4,2,16,2,512]{5,4,3,2,1,0:T(2,128)} %copy.58) | data formatting | bytes 2097152 | tf_op jit(solution)/shard_map/reshape | solution.py:154
  141.3 4.3 %convolution_convert_fusion = bf16[2048,1024]{1,0:T(8,128)(2,1)} fusion(bf16[128,1024]{1,0:T(8,128)(2,1)S(1)} %get-tuple-element.31, f32[128,2048]{1,0:T(8,128)S(1)} %reshape.220, f32[2048]{0:T(1024)S(1)} %copy-done.27, f32[128]{0:T(128)} %copy-done.31, f32[128]{0:T(128)} %div.75), kind=kOutput, calls=%fused_computation.12 | convolution fusion | flops 540016640 | bytes 5514240 | tf_op jit(solution)/shard_map/dot_general | solution.py:172
  152.0 2.1 reshape_reshape.30
  154.1 2.8 %copy.62 = bf16[4,16,32,128]{3,2,1,0:T(8,128)(2,1)S(1)} copy(bf16[4,16,32,128]{2,1,3,0:T(8,128)(2,1)} %bitcast.129) | data formatting | bytes 1048576 | tf_op jit(solution)/shard_map/transpose(jvp(whqk,wkhd->wqhd))/transpose | solution.py:60
  156.9 2.8 %fusion.13 = bf16[4,128,1,16,32]{1,4,3,0,2:T(8,128)(2,1)S(1)} fusion(bf16[4,16,32,128]{3,2,1,0:T(8,128)(2,1)S(1)} %copy.62, bf16[4,16,128,128]{2,3,1,0:T(8,128)(2,1)} %copy-done.1), kind=kOutput, calls=%fused_computation.37 | convolution fusion | flops 67371008 | bytes 3145728 | tf_op jit(solution)/shard_map/transpose(jvp(whqk,wkhd->wqhd))/dot_general | solution.py:60
  159.7 3.4 %fusion.6 = (f32[4,16,128]{2,1,0:T(8,128)S(1)}, bf16[4,16,128,128]{2,3,1,0:T(8,128)(2,1)S(1)}) fusion(f32[4,16,128,128]{2,3,1,0:T(8,128)} %copy-done.2, f32[4,16,128]{2,1,0:T(8,128)S(1)} %multiply_divide_fusion, bf16[4,16,32,128]{3,2,1,0:T(8,128)(2,1)S(1)} %copy.62, bf16[4,128,1,16,32]{1,4,3,0,2:T(8,128)(2,1)S(1)} %copy-done.8), kind=kOutput, calls=%fused_computation.8 | convolution fusion | flops 72343552 | bytes 7405568 | tf_op jit(solution)/shard_map/transpose(jvp(whqk,wkhd->wqhd))/dot_general | solution.py:60
  167.0 7.4 %copy.67 = bf16[4,128,3,16,32]{4,3,2,1,0:T(8,128)(2,1)} copy(bf16[4,128,3,16,32]{1,4,3,0,2:T(8,128)(2,1)} %pad_maximum_fusion.1) | data formatting | bytes 3145728 | tf_op jit(solution)/shard_map/stack | solution.py:124
  174.4 9.3 %reshape_reshape.31 = bf16[1,4,2,8,8,1536]{5,4,3,2,1,0:T(8,128)(2,1)} reshape(bf16[4,128,3,16,32]{4,3,2,1,0:T(8,128)(2,1)} %copy.67) | data formatting | bytes 3145728 | tf_op jit(solution)/shard_map/reshape;reshape | solution.py:39
  190.6 4.0 %collective-permute-done.6 = bf16[2,7,32,512]{3,2,1,0:T(8,128)(2,1)S(1)} collective-permute-done((bf16[2,7,32,512]{3,2,1,0:T(8,128)(2,1)S(1)}, bf16[2,7,32,512]{3,2,1,0:T(8,128)(2,1)S(1)}, u32[]{:S(2)}, u32[]{:S(2)}) %collective-permute-start.6) | collective-permute-done | bytes 458784 | tf_op jit(solution)/shard_map/ppermute | solution.py:19
  196.4 54.0 %reduce_gradients.1 = (f32[8,1536]{1,0:T(8,128)}, f32[8,512]{1,0:T(8,128)}, f32[32,1024]{1,0:T(8,128)}, f32[16,2048]{1,0:T(8,128)}) custom-call(bf16[4,2,4,16,2048]{4,3,2,1,0:T(8,128)(2,1)} %pad_maximum_fusion.at_ref, bf16[4,2,4,32,2048]{4,3,2,1,0:T(8,128)(2,1)} %bitcast.127, bf16[4,2,4,64,1024]{4,3,2,1,0:T(8,128)(2,1)} %bitcast.128), custom_call_target="tpu_custom_call" | custom-call | tf_op jit(solution)/shard_map/reduce_gradients/pallas_call | solution.py:468
  (161 shorter events, 72.9 us)
Async XLA Ops:
  0.6 21.6 %copy-start = (bf16[512,1536]{1,0:T(8,128)(2,1)S(1)}, bf16[512,1536]{1,0:T(8,128)(2,1)}, u32[]{:S(2)}) copy-start(bf16[512,1536]{1,0:T(8,128)(2,1)} %param.16) | copy-start | bytes 4718596
  0.6 20.4 %copy-start.29 = (f32[512]{0:T(512)S(1)}, f32[512]{0:T(512)}, u32[]{:S(2)}) copy-start(f32[512]{0:T(512)} %param.15) | copy-start | bytes 6148
  1.8 11.4 %collective-permute-start = (bf16[2,7,32,512]{3,2,1,0:T(8,128)(2,1)S(1)}, bf16[2,7,32,512]{3,2,1,0:T(8,128)(2,1)S(1)}, u32[]{:S(2)}, u32[]{:S(2)}) collective-permute-start(bf16[2,7,32,512]{3,2,1,0:T(8,128)(2,1)S(1)} %slice.42), channel_id=1, source_target_pairs={{0,112},{16,0},{32,16},{48,32},{64,48},{80,64},{96,80},{112,96},{1... | collective-permute-start | bytes 1376264 | tf_op jit(solution)/shard_map/ppermute | solution.py:19
  14.4 5.9 %collective-permute-start.1 = (bf16[2,8,7,512]{3,2,1,0:T(8,128)(2,1)S(1)}, bf16[2,8,7,512]{3,2,1,0:T(8,128)(2,1)S(1)}, u32[]{:S(2)}, u32[]{:S(2)}) collective-permute-start(bf16[2,8,7,512]{3,2,1,0:T(8,128)(2,1)S(1)} %slice.55), channel_id=1, source_target_pairs={{0,14},{2,0},{4,2},{6,4},{8,6},{10,8},{12,10},{14,12},{1,15},{3,1}... | collective-permute-start | bytes 344072 | tf_op jit(solution)/shard_map/ppermute | solution.py:19
  41.7 8.4 %copy-start.21 = (bf16[4,128,1,16,32]{1,4,3,0,2:T(8,128)(2,1)}, bf16[4,128,1,16,32]{1,4,3,0,2:T(8,128)(2,1)S(1)}, u32[]{:S(2)}) copy-start(bf16[4,128,1,16,32]{1,4,3,0,2:T(8,128)(2,1)S(1)} %copy.79) | copy-start | bytes 1572868
  48.1 7.1 %copy-start.7 = (bf16[4,128,1,16,32]{1,4,3,0,2:T(8,128)(2,1)}, bf16[4,128,1,16,32]{1,4,3,0,2:T(8,128)(2,1)S(1)}, u32[]{:S(2)}) copy-start(bf16[4,128,1,16,32]{1,4,3,0,2:T(8,128)(2,1)S(1)} %copy.77) | copy-start | bytes 1572868
  57.2 16.4 %copy-start.12 = (bf16[2,8,32,512]{3,2,1,0:T(8,128)(2,1)S(1)}, bf16[2,8,32,512]{3,2,1,0:T(8,128)(2,1)}, u32[]{:S(2)}) copy-start(bf16[2,8,32,512]{3,2,1,0:T(8,128)(2,1)} %param.12) | copy-start | bytes 1572868
  68.0 18.1 %collective-permute-start.2 = (bf16[2,7,32,512]{3,2,1,0:T(8,128)(2,1)}, bf16[2,7,32,512]{3,2,1,0:T(8,128)(2,1)}, u32[]{:S(2)}, u32[]{:S(2)}) collective-permute-start(bf16[2,7,32,512]{3,2,1,0:T(8,128)(2,1)} %slice.59), channel_id=1, source_target_pairs={{0,16},{16,32},{32,48},{48,64},{64,80},{80,96},{96,112},{112,0},{1... | collective-permute-start | bytes 1376264 | tf_op jit(solution)/shard_map/ppermute | solution.py:19
  78.2 9.1 %copy-start.9 = (bf16[128,2048]{1,0:T(8,128)(2,1)}, bf16[128,2048]{1,0:T(8,128)(2,1)S(1)}, u32[]{:S(2)}) copy-start(bf16[128,2048]{1,0:T(8,128)(2,1)S(1)} %reshape.212) | copy-start | bytes 1572868
  87.4 8.2 %collective-permute-start.3 = (bf16[2,8,7,512]{3,2,1,0:T(8,128)(2,1)S(1)}, bf16[2,8,7,512]{3,2,1,0:T(8,128)(2,1)S(1)}, u32[]{:S(2)}, u32[]{:S(2)}) collective-permute-start(bf16[2,8,7,512]{3,2,1,0:T(8,128)(2,1)S(1)} %slice.60), channel_id=1, source_target_pairs={{0,2},{2,4},{4,6},{6,8},{8,10},{10,12},{12,14},{14,0},{1,3},{3,5},... | collective-permute-start | bytes 344072 | tf_op jit(solution)/shard_map/ppermute | solution.py:19
  97.9 7.8 %copy-start.27 = (f32[2048]{0:T(1024)S(1)}, f32[2048]{0:T(1024)}, u32[]{:S(2)}) copy-start(f32[2048]{0:T(1024)} %param.19) | copy-start | bytes 24580
  105.7 3.6 %copy-start.4 = (bf16[1024,2048]{1,0:T(8,128)(2,1)S(1)}, bf16[1024,2048]{1,0:T(8,128)(2,1)}, u32[]{:S(2)}) copy-start(bf16[1024,2048]{1,0:T(8,128)(2,1)} %param.21) | copy-start | bytes 12582916
  105.7 8.1 %copy-start.31 = (f32[128]{0:T(128)}, f32[128]{0:T(128)S(1)}, u32[]{:S(2)}) copy-start(f32[128]{0:T(128)S(1)} %rsqrt.30) | copy-start | bytes 1540
  109.3 2.8 %copy-start.17 = (bf16[2048,1024]{1,0:T(8,128)(2,1)S(1)}, bf16[2048,1024]{1,0:T(8,128)(2,1)}, u32[]{:S(2)}) copy-start(bf16[2048,1024]{1,0:T(8,128)(2,1)} %param.20) | copy-start | bytes 12582916
  109.3 2.8 %copy-start.28 = (f32[128]{0:T(128)S(1)}, f32[128]{0:T(128)}, u32[]{:S(2)}) copy-start(f32[128]{0:T(128)} %div.75) | copy-start | bytes 1540
  127.2 18.3 %collective-permute-start.4 = (bf16[2,7,32,512]{3,2,1,0:T(8,128)(2,1)}, bf16[2,7,32,512]{3,2,1,0:T(8,128)(2,1)}, u32[]{:S(2)}, u32[]{:S(2)}) collective-permute-start(bf16[2,7,32,512]{3,2,1,0:T(8,128)(2,1)} %slice.61), channel_id=1, source_target_pairs={{0,112},{16,0},{32,16},{48,32},{64,48},{80,64},{96,80},{112,96},{1... | collective-permute-start | bytes 1376264 | tf_op jit(solution)/shard_map/ppermute | solution.py:19
  141.3 4.3 %copy-start.16 = (bf16[2,8,32,512]{3,2,1,0:T(8,128)(2,1)S(1)}, bf16[2,8,32,512]{3,2,1,0:T(8,128)(2,1)}, u32[]{:S(2)}) copy-start(bf16[2,8,32,512]{3,2,1,0:T(8,128)(2,1)} %copy-done.15) | copy-start | bytes 1572868
  141.3 7.2 %copy-start.5 = (f32[2,8,32,512]{3,2,1,0:T(8,128)S(1)}, f32[2,8,32,512]{3,2,1,0:T(8,128)}, u32[]{:S(2)}) copy-start(f32[2,8,32,512]{3,2,1,0:T(8,128)} %fusion.32) | copy-start | bytes 3145732
  141.3 7.2 %copy-start.18 = (f32[2,8,32,512]{3,2,1,0:T(8,128)S(1)}, f32[2,8,32,512]{3,2,1,0:T(8,128)}, u32[]{:S(2)}) copy-start(f32[2,8,32,512]{3,2,1,0:T(8,128)} %reshape.210) | copy-start | bytes 3145732
  141.3 9.9 %copy-start.20 = (bf16[512,512]{1,0:T(8,128)(2,1)S(1)}, bf16[512,512]{1,0:T(8,128)(2,1)}, u32[]{:S(2)}) copy-start(bf16[512,512]{1,0:T(8,128)(2,1)} %param.17) | copy-start | bytes 1572868
  146.7 4.1 %collective-permute-start.5 = (bf16[2,8,7,512]{3,2,1,0:T(8,128)(2,1)S(1)}, bf16[2,8,7,512]{3,2,1,0:T(8,128)(2,1)S(1)}, u32[]{:S(2)}, u32[]{:S(2)}) collective-permute-start(bf16[2,8,7,512]{3,2,1,0:T(8,128)(2,1)S(1)} %slice.62), channel_id=1, source_target_pairs={{0,14},{2,0},{4,2},{6,4},{8,6},{10,8},{12,10},{14,12},{1,15},{3,1}... | collective-permute-start | bytes 344072 | tf_op jit(solution)/shard_map/ppermute | solution.py:19
  152.0 7.7 %copy-start.8 = (bf16[4,128,1,16,32]{1,4,3,0,2:T(8,128)(2,1)S(1)}, bf16[4,128,1,16,32]{1,4,3,0,2:T(8,128)(2,1)}, u32[]{:S(2)}) copy-start(bf16[4,128,1,16,32]{1,4,3,0,2:T(8,128)(2,1)} %copy-done.7) | copy-start | bytes 1572868
  159.7 3.5 %copy-start.3 = (f32[4,16,128,128]{2,3,1,0:T(8,128)S(1)}, f32[4,16,128,128]{2,3,1,0:T(8,128)}, u32[]{:S(2)}) copy-start(f32[4,16,128,128]{2,3,1,0:T(8,128)} %copy-done.2) | copy-start | bytes 12582916
  159.7 3.6 %copy-start.23 = (bf16[4,128,1,16,32]{1,4,3,0,2:T(8,128)(2,1)S(1)}, bf16[4,128,1,16,32]{1,4,3,0,2:T(8,128)(2,1)}, u32[]{:S(2)}) copy-start(bf16[4,128,1,16,32]{1,4,3,0,2:T(8,128)(2,1)} %copy.78) | copy-start | bytes 1572868
  174.4 10.8 %copy-start.30 = (f32[512]{0:T(512)S(1)}, f32[512]{0:T(512)}, u32[]{:S(2)}) copy-start(f32[512]{0:T(512)} %param.15) | copy-start | bytes 6148
  185.3 3.9 %copy-start.11 = (bf16[2,8,32,512]{3,2,1,0:T(8,128)(2,1)S(1)}, bf16[2,8,32,512]{3,2,1,0:T(8,128)(2,1)}, u32[]{:S(2)}) copy-start(bf16[2,8,32,512]{3,2,1,0:T(8,128)(2,1)} %copy-done.10) | copy-start | bytes 1572868
  185.3 3.9 %copy-start.24 = (bf16[512,512]{1,0:T(8,128)(2,1)S(1)}, bf16[512,512]{1,0:T(8,128)(2,1)}, u32[]{:S(2)}) copy-start(bf16[512,512]{1,0:T(8,128)(2,1)} %copy.70) | copy-start | bytes 1572868
  186.4 3.2 %copy-start.26 = (bf16[512,512]{1,0:T(8,128)(2,1)S(1)}, bf16[512,512]{1,0:T(8,128)(2,1)}, u32[]{:S(2)}) copy-start(bf16[512,512]{1,0:T(8,128)(2,1)} %copy.69) | copy-start | bytes 1572868
  187.0 7.5 %collective-permute-start.6 = (bf16[2,7,32,512]{3,2,1,0:T(8,128)(2,1)S(1)}, bf16[2,7,32,512]{3,2,1,0:T(8,128)(2,1)S(1)}, u32[]{:S(2)}, u32[]{:S(2)}) collective-permute-start(bf16[2,7,32,512]{3,2,1,0:T(8,128)(2,1)S(1)} %slice.63), channel_id=1, source_target_pairs={{0,16},{16,32},{32,48},{48,64},{64,80},{80,96},{96,112},{112,0},{1... | collective-permute-start | bytes 1376264 | tf_op jit(solution)/shard_map/ppermute | solution.py:19
  194.8 55.7 %collective-permute-start.7 = (bf16[2,8,7,512]{3,2,1,0:T(8,128)(2,1)S(1)}, bf16[2,8,7,512]{3,2,1,0:T(8,128)(2,1)S(1)}, u32[]{:S(2)}, u32[]{:S(2)}) collective-permute-start(bf16[2,8,7,512]{3,2,1,0:T(8,128)(2,1)S(1)} %slice.64), channel_id=1, source_target_pairs={{0,2},{2,4},{4,6},{6,8},{8,10},{10,12},{12,14},{14,0},{1,3},{3,5},... | collective-permute-start | bytes 344072 | tf_op jit(solution)/shard_map/ppermute | solution.py:19
  196.4 54.0 %copy-start.6 = (f32[2,8,32,512]{3,2,1,0:T(8,128)S(1)}, f32[2,8,32,512]{3,2,1,0:T(8,128)}, u32[]{:S(2)}) copy-start(f32[2,8,32,512]{3,2,1,0:T(8,128)} %reshape.214) | copy-start | bytes 3145732
  196.4 54.0 %copy-start.13 = (bf16[2,8,32,512]{3,2,1,0:T(8,128)(2,1)S(1)}, bf16[2,8,32,512]{3,2,1,0:T(8,128)(2,1)}, u32[]{:S(2)}) copy-start(bf16[2,8,32,512]{3,2,1,0:T(8,128)(2,1)} %param.12) | copy-start | bytes 1572868
  (10 other events, 12.7 us)

commit v2 on v1

v2 whole, which is shorter than its diff:
```python
import jax
import jax.numpy as jnp
from jax import lax
from jax.experimental import pallas as pl
from jax.experimental.pallas import tpu as pltpu
from jax.sharding import PartitionSpec as P

epsilon = 1e-05

MESH = pl.DeviceIdType.MESH


class Ring:
    def __init__(self, place, right, left, block, store, bufs, send_sems, recv_sems, lead, half):
        self.place, self.right, self.left = place, right, left
        self.block, self.store = block, store
        self.bufs, self.outs = bufs[0], bufs[1]
        self.send_sems, self.recv_sems = send_sems, recv_sems
        self.lead, self.half = lead, half
        self.copies = {}

    def part(self, k, which):
        return self.block(k).at[:, :, pl.ds(which * self.half, self.half)]

    def copy(self, slot, source, target):
        made = pltpu.make_async_remote_copy(
            src_ref=source,
            dst_ref=self.bufs.at[slot],
            send_sem=self.send_sems.at[slot],
            recv_sem=self.recv_sems.at[slot],
            device_id=target,
            device_id_type=MESH,
        )
        made.start()
        self.copies[slot] = made

    def begin(self):
        ahead = lax.rem(self.place + 1, 4)
        across = lax.rem(self.place + 2, 4)
        behind = lax.rem(self.place + 3, 4)
        self.copy(0, self.part(across, 0), self.right)
        self.copy(3, self.part(across, 1), self.left)
        self.copy(1, self.part(ahead, 1), self.right)
        self.copy(4, self.part(behind, 0), self.left)

    def middle(self):
        ahead = lax.rem(self.place + 1, 4)
        behind = lax.rem(self.place + 3, 4)
        for slot, which, k, out, target in ((0, 0, ahead, 0, self.right), (3, 1, behind, 1, self.left)):
            self.copies[slot].wait_recv()

            def add(i, carry, slot=slot, which=which, k=k, out=out):
                mine = self.block(k)[i, :, pl.ds(which * self.half, self.half)]
                total = mine.astype(jnp.float32) + self.bufs[slot, i].astype(jnp.float32)
                self.outs[out, i] = total.astype(jnp.bfloat16)
                return carry

            lax.fori_loop(0, self.lead, add, 0)
            self.copy(2 if out == 0 else 5, self.outs.at[out], target)

    def finish(self):
        for slot in (1, 2, 4, 5):
            self.copies[slot].wait_recv()

        def add(i, carry):
            for which, first, second in ((0, 2, 4), (1, 5, 1)):
                mine = self.block(self.place)[i, :, pl.ds(which * self.half, self.half)]
                total = (
                    mine.astype(jnp.float32)
                    + self.bufs[first, i].astype(jnp.float32)
                    + self.bufs[second, i].astype(jnp.float32)
                )
                self.store(i, which, total)
            return carry

        lax.fori_loop(0, self.lead, add, 0)

    def drain(self):
        for slot in range(6):
            self.copies[slot].wait_send()


class Stream:
    def __init__(self, where, source, first_axis, scratch, store):
        red, buf1, out1, buf2, out2, fin, zsend, zrecv, ssem, rsem = scratch
        self.where, self.scratch, self.store = where, scratch, store
        self.rows, self.width = source.shape[2], source.shape[3]
        half = self.width // 2
        axes = {
            "y": (where["y"], where["up"], where["down"], lambda k: source.at[k]),
            "x": (where["x"], where["east"], where["west"], lambda k: source.at[:, k]),
        }
        second_axis = "x" if first_axis == "y" else "y"

        def store_red(i, which, total):
            red[i, 0, :, pl.ds(which * half, half)] = total.astype(jnp.bfloat16)

        def store_fin(i, which, total):
            deep = self.rows // 2
            for z in range(2):
                fin[z, :, pl.ds(which * half, half)] = total[z * deep : (z + 1) * deep]

        place, right, left, block = axes[first_axis]
        self.ring1 = Ring(
            place, right, left, block, store_red, (buf1, out1), ssem.at[pl.ds(0, 6)], rsem.at[pl.ds(0, 6)], 4, half
        )
        place, right, left, _unused = axes[second_axis]
        self.ring2 = Ring(
            place,
            right,
            left,
            lambda k: red.at[k],
            store_fin,
            (buf2, out2),
            ssem.at[pl.ds(6, 6)],
            rsem.at[pl.ds(6, 6)],
            1,
            half,
        )

    def z_begin(self):
        _r, _a, _b, _c, _d, fin, zsend, zrecv, ssem, rsem = self.scratch
        zsend[...] = fin[1 - self.where["z"]].astype(zsend.dtype)
        self.z_copy = pltpu.make_async_remote_copy(
            src_ref=zsend,
            dst_ref=zrecv,
            send_sem=ssem.at[12],
            recv_sem=rsem.at[12],
            device_id=self.where["beside"],
            device_id_type=MESH,
        )
        self.z_copy.start()

    def z_finish(self):
        fin, zrecv = self.scratch[5], self.scratch[7]
        self.z_copy.wait_recv()
        self.store(fin[self.where["z"]] + zrecv[...].astype(jnp.float32))

    def drain(self):
        self.ring1.drain()
        self.ring2.drain()
        self.z_copy.wait_send()


def stream_scratch(rows, width, z_type):
    half = width // 2
    deep = rows // 2
    return [
        pltpu.VMEM((4, 1, rows, width), jnp.bfloat16),
        pltpu.VMEM((6, 4, rows, half), jnp.bfloat16),
        pltpu.VMEM((2, 4, rows, half), jnp.bfloat16),
        pltpu.VMEM((6, 1, rows, half), jnp.bfloat16),
        pltpu.VMEM((2, 1, rows, half), jnp.bfloat16),
        pltpu.VMEM((2, deep, width), jnp.float32),
        pltpu.VMEM((deep, width), z_type),
        pltpu.VMEM((deep, width), z_type),
        pltpu.SemaphoreType.DMA((13,)),
        pltpu.SemaphoreType.DMA((13,)),
    ]


def places():
    lat, lon = lax.axis_index("lat"), lax.axis_index("lon")
    core, z = lax.rem(lat, 2), lax.rem(lon, 2)
    return {
        "lat": lat,
        "lon": lon,
        "y": lat // 2,
        "x": lon // 2,
        "core": core,
        "z": z,
        "up": {"lat": lax.rem(lat + 2, 8)},
        "down": {"lat": lax.rem(lat + 6, 8)},
        "east": {"lon": lax.rem(lon + 2, 8)},
        "west": {"lon": lax.rem(lon + 6, 8)},
        "beside": {"lon": lon + 1 - 2 * z},
        "sibling": {"lat": lat + 1 - 2 * core},
    }


def dot(a, b):
    return lax.dot_general(a, b, (((1,), (0,)), ((), ())), preferred_element_type=jnp.float32)


def dot_nt(a, b):
    return lax.dot_general(a, b, (((1,), (1,)), ((), ())), preferred_element_type=jnp.float32)


def dot_tn(a, b):
    return lax.dot_general(a, b, (((0,), (0,)), ((), ())), preferred_element_type=jnp.float32)


def code_of(row, col):
    return (row + 16) * 64 + (col + 16)


def fine_code(s):
    return code_of(s >> 5, s & 31)


def patch_code(s):
    quarter, coarse = s >> 6, s & 63
    return code_of(2 * (coarse >> 4) + (quarter >> 1), 2 * (coarse & 15) + (quarter & 1))


def window_code(s):
    return code_of((s & 63) >> 3, 8 * (s >> 6) + (s & 7))


def rim_code(t):
    kind, c4 = t >> 5, t & 3
    row = jnp.where(kind < 2, (t & 31) >> 2, ((t & 15) >> 2) + jnp.where(kind == 2, 8, -4))
    west = jnp.where(kind < 2, kind & 1, (t >> 4) & 1)
    return code_of(row, c4 + 32 - 36 * west)


def iota(shape, axis):
    return lax.broadcasted_iota(jnp.int32, shape, axis)


def one_hot(same):
    return jnp.where(same, 1.0, 0.0).astype(jnp.bfloat16)


def fill_gather(ref, target_code, source_code, offset):
    target = target_code(iota((256, 128), 0)) + offset
    lane = iota((1, 128), 1)
    half = (lane >> 5 << 6) + (lane & 31)
    pieces = (
        source_code(lane),
        source_code(lane + 128),
        source_code(half + 32) - 8 * 64,
        source_code(half) + 8 * 64,
        rim_code(lane),
    )
    for n, piece in enumerate(pieces):
        ref[:, n * 128 : (n + 1) * 128] = one_hot(target == piece)


def fill_pack(ref, source_code):
    t = iota((64, 256), 0)
    target = code_of((t & 31) >> 2, (t & 3) + jnp.where(t >= 32, 28, 0))
    ref[...] = one_hot(target == source_code(iota((1, 256), 1)))


class Exchange:
    def __init__(self, where, source, pack, scratch):
        self.where, self.source, self.pack = where, source, pack
        self.packed, self.north, self.south, self.rim, self.ssem, self.rsem = scratch
        self.copies = []

    def copy(self, source, target, lat, lon):
        n = len(self.copies)
        made = pltpu.make_async_remote_copy(
            src_ref=source,
            dst_ref=target,
            send_sem=self.ssem.at[n],
            recv_sem=self.rsem.at[n],
            device_id={
                "lat": lax.rem(self.where["lat"] + lat + 8, 8),
                "lon": lax.rem(self.where["lon"] + lon + 8, 8),
            },
            device_id_type=MESH,
        )
        made.start()
        self.copies.append(made)

    def begin(self):
        first, last = pl.ds(0, 32), pl.ds(32, 32)
        self.copy(self.source.at[:, :, first], self.south, -1, 0)
        self.copy(self.source.at[:, :, last], self.north, 1, 0)
        for level in range(2):
            rim = dot(self.pack[...], self.source[:, level].reshape(256, 512)).astype(jnp.bfloat16)
            self.packed[0, level] = rim[:32]
            self.packed[1, level] = rim[32:]
        self.copy(self.packed.at[0], self.rim.at[:, pl.ds(0, 32)], 0, -1)
        self.copy(self.packed.at[1], self.rim.at[:, pl.ds(32, 32)], 0, 1)
        near, far = pl.ds(0, 16), pl.ds(16, 16)
        self.copy(self.packed.at[0, :, near], self.rim.at[:, pl.ds(64, 16)], -1, -1)
        self.copy(self.packed.at[1, :, near], self.rim.at[:, pl.ds(80, 16)], -1, 1)
        self.copy(self.packed.at[0, :, far], self.rim.at[:, pl.ds(96, 16)], 1, -1)
        self.copy(self.packed.at[1, :, far], self.rim.at[:, pl.ds(112, 16)], 1, 1)

    def arrive(self):
        for made in self.copies:
            made.wait_recv()

    def gather(self, level, moves):
        cells = jnp.concatenate(
            (
                self.source[:, level].reshape(256, 512),
                self.north[:, level].reshape(128, 512),
                self.south[:, level].reshape(128, 512),
                self.rim[level],
            ),
            axis=0,
        )
        return dot(moves[...], cells)

    def drain(self):
        for made in self.copies:
            made.wait_send()


def exchange_scratch():
    bf16 = jnp.bfloat16
    return [
        pltpu.VMEM((2, 2, 32, 512), bf16),
        pltpu.VMEM((4, 2, 32, 512), bf16),
        pltpu.VMEM((4, 2, 32, 512), bf16),
        pltpu.VMEM((2, 128, 512), bf16),
        pltpu.SemaphoreType.DMA((8,)),
        pltpu.SemaphoreType.DMA((8,)),
    ]


def send(source, target, ssem, rsem, device):
    made = pltpu.make_async_remote_copy(
        src_ref=source, dst_ref=target, send_sem=ssem, recv_sem=rsem, device_id=device, device_id_type=MESH
    )
    made.start()
    return made


def block_kernel(
    shifts_ref,
    bias_ref,
    fine_ref,
    cot_ref,
    land_ref,
    gain_attn_ref,
    gain_merge_ref,
    w_qkv_hbm,
    w_proj_hbm,
    w_merge_hbm,
    w_expand_hbm,
    out_ref,
    field_ref,
    qkv_out,
    proj_out,
    mg_out,
    ex_out,
    *scratch,
):
    scratch = list(scratch)

    def take(n):
        got = scratch[:n]
        del scratch[:n]
        return got

    f32, bf16 = jnp.float32, jnp.bfloat16
    w_qkv, w_proj, w_merge, w_expand, wsem = take(5)
    to_window, to_patch, pack_patch, pack_window = take(4)
    x_patch, c_patch, normed_w, hat_w, rstd_w = take(5)
    qkv, weights, attended, branch = take(4)
    hidden, hat_m, rstd_m, merged, slope, act, gcoarse, out_patch, ghidden, gbranch = take(10)
    sib_cot, sib_act, sib_merged, sib_gcoarse, fsem, frsem = take(6)
    gbranch_w, gattended, gqkv, grolled, normed_t, attended_t, at_source = take(7)
    acc_at1, acc_at2, acc_ex, acc_mg, got_at, asem, arsem = take(7)
    exchanges = [take(6) for _ in range(4)]
    streams_scratch = [take(10) for _ in range(4)]

    where = places()
    core, lat, lon = where["core"], where["lat"], where["lon"]
    loads = []
    for n, (far, near) in enumerate(
        ((w_qkv_hbm, w_qkv), (w_proj_hbm, w_proj), (w_merge_hbm, w_merge), (w_expand_hbm, w_expand))
    ):
        made = pltpu.make_async_copy(far, near, wsem.at[n])
        made.start()
        loads.append(made)

    barrier = pltpu.get_barrier_semaphore()
    around = [(a, b) for a in (-1, 0, 1) for b in (-1, 0, 1) if (a, b) != (0, 0)]
    around += [(2, 0), (-2, 0), (0, 2), (0, -2)]
    for a, b in around:
        pl.semaphore_signal(
            barrier,
            inc=1,
            device_id={"lat": lax.rem(lat + a + 8, 8), "lon": lax.rem(lon + b + 8, 8)},
            device_id_type=MESH,
        )

    shift_lat, shift_lon = shifts_ref[0], shifts_ref[1]
    low_lat = shift_lat <= 4
    off_lat = jnp.where(low_lat, shift_lat, shift_lat - 8)
    off_lon = jnp.where(shift_lon <= 4, shift_lon, shift_lon - 8)
    offset = off_lat * 64 + off_lon

    fill_pack(pack_patch, patch_code)
    arrange_hot = one_hot(patch_code(iota((256, 256), 0)) == fine_code(iota((1, 256), 1)))
    for source, target in ((fine_ref, x_patch), (cot_ref, c_patch)):
        for level in range(2):
            target[:, level] = dot(arrange_hot, source[level]).astype(bf16).reshape(4, 64, 512)
    pl.semaphore_wait(barrier, len(around))

    first = Exchange(where, x_patch, pack_patch, exchanges[0])
    first.begin()
    factors = [send(c_patch, sib_cot, fsem.at[0], frsem.at[0], where["sibling"])]

    fill_gather(to_window, window_code, patch_code, offset)
    fill_gather(to_patch, patch_code, window_code, -offset)
    fill_pack(pack_window, window_code)

    (land_keys,) = take(1)

    def land_window(w, carry):
        key = iota((256, 128), 1)
        col_at = (32 * lon + off_lon + 8 * w + (key & 7) + 256) & 255
        land_cols = dot(land_ref[...].astype(bf16), one_hot(iota((256, 128), 0) == col_at))
        key = iota((64, 128), 1)
        row_at = (8 * lat + off_lat + ((key & 63) >> 3) + 64) & 63
        land_keys[w] = jnp.sum(jnp.where(iota((64, 128), 0) == row_at, land_cols, 0.0), axis=0, keepdims=True)
        return carry

    lax.fori_loop(0, 4, land_window, 0)

    band = jnp.where(low_lat, lat, lax.rem(lat + 7, 8))

    def region(cell):
        row = 8 * band + ((cell & 63) >> 3)
        return jnp.where(row >= 56, 1, 0) + jnp.where(row >= 64 - shift_lat, 1, 0)

    same_region = region(iota((128, 128), 0)) == region(iota((128, 128), 1))
    heads = [jnp.where(iota((1, 128), 1) >> 5 == h, 1.0, 0.0).astype(bf16) for h in range(4)]

    def head_stack(value):
        return jnp.concatenate([value * head for head in heads], axis=0)

    def head_row(stack):
        return jnp.concatenate([stack[h * 128 : (h + 1) * 128] for h in range(4)], axis=1)

    gain_attn = gain_attn_ref[...]
    first.arrive()
    for level in range(2):
        cells = first.gather(level, to_window)
        average = jnp.mean(cells, axis=-1, keepdims=True)
        centred = cells - average
        rstd = lax.rsqrt(jnp.mean(centred * centred, axis=-1, keepdims=True) + epsilon)
        hat = centred * rstd
        hat_w[:, level] = hat.reshape(4, 64, 512)
        rstd_w[:, level] = jnp.broadcast_to(rstd, (256, 128)).reshape(4, 64, 128)
        normed_w[:, level] = (hat * gain_attn).astype(bf16).reshape(4, 64, 512)

    loads[0].wait()
    normed = normed_w[...].reshape(512, 512)

    def project(n, carry):
        cols = w_qkv[:, pl.ds(pl.multiple_of(n * 256, 256), 256)]
        got = dot(normed_w[...].reshape(512, 512), cols).astype(bf16)
        for part in range(2):
            qkv[2 * n + part] = got[:, part * 128 : (part + 1) * 128].reshape(4, 128, 128)
        return carry

    lax.fori_loop(0, 6, project, 0)
    normed_t[...] = normed.T

    scale = 32.0 ** (-0.5)

    def attend(n, carry):
        w, g = n >> 2, n & 3
        scores = dot_nt(head_stack(qkv[g, w]), qkv[4 + g, w])
        land = land_keys[w]
        parts = []
        for h in range(4):
            score = scores[h * 128 : (h + 1) * 128] * scale + bias_ref[4 * g + h] * land
            score = jnp.where(same_region, score, -1000000000.0)
            raised = jnp.exp(score - jnp.max(score, axis=-1, keepdims=True))
            parts.append((raised / jnp.sum(raised, axis=-1, keepdims=True)).astype(bf16))
        weights[w, g] = jnp.concatenate(parts, axis=0)
        mixed = dot(jnp.concatenate(parts, axis=1), head_stack(qkv[8 + g, w]))
        attended[w, :, pl.ds(pl.multiple_of(g * 128, 128), 128)] = mixed.astype(bf16)
        return carry

    lax.fori_loop(0, 16, attend, 0)

    loads[1].wait()
    mixed_all = attended[...].reshape(512, 512)
    branch[...] = dot(mixed_all, w_proj[...]).astype(bf16).reshape(4, 2, 64, 512)
    second = Exchange(where, branch, pack_window, exchanges[1])
    second.begin()
    attended_t[...] = mixed_all.T
    second.arrive()
    for level in range(2):
        back = second.gather(level, to_patch).reshape(4, 64, 512)
        hidden[:, level] = (x_patch[:, level].astype(f32) + back.astype(bf16).astype(f32)).astype(bf16)

    def patches(ref):
        return jnp.concatenate([ref[q].reshape(128, 512) for q in range(4)], axis=1)

    gain_merge = gain_merge_ref[...]
    cells = patches(hidden).astype(f32)
    average = jnp.mean(cells, axis=-1, keepdims=True)
    centred = cells - average
    rstd = lax.rsqrt(jnp.mean(centred * centred, axis=-1, keepdims=True) + epsilon)
    hat = centred * rstd
    hat_m[...] = hat
    rstd_m[...] = jnp.broadcast_to(rstd, (128, 128))
    scaled = (hat * gain_merge).astype(bf16)
    for q in range(4):
        merged[q] = scaled[:, q * 512 : (q + 1) * 512]
    other = pl.multiple_of((1 - core) * 256, 256)
    factors.append(send(merged.at[:, :, pl.ds(other, 256)], sib_merged, fsem.at[1], frsem.at[1], where["sibling"]))

    loads[2].wait()
    bend = 0.7978845608028654

    def merge(n, carry):
        rows = jnp.concatenate([merged[q] for q in range(4)], axis=1)
        coarse = dot(rows, w_merge[:, pl.ds(pl.multiple_of(n * 256, 256), 256)])
        square = coarse * coarse
        bent = jnp.tanh(bend * (coarse + 0.044715 * (coarse * square)))
        act[n] = (0.5 * coarse * (1.0 + bent)).astype(bf16)
        inner = bend * (1.0 + 3.0 * 0.044715 * square)
        slope[n] = 0.5 * (1.0 + bent) + 0.5 * coarse * (1.0 - bent * bent) * inner
        return carry

    lax.fori_loop(0, 4, merge, 0)
    other = pl.multiple_of((1 - core) * 128, 128)
    factors.append(send(act.at[:, :, pl.ds(other, 128)], sib_act, fsem.at[2], frsem.at[2], where["sibling"]))

    loads[3].wait()

    def back_expand(n, carry):
        rows = patches(c_patch)
        slab = w_expand[pl.ds(pl.multiple_of(n * 256, 256), 256), :]
        gcoarse[n] = (slope[n] * dot_nt(rows, slab)).astype(bf16)
        return carry

    lax.fori_loop(0, 4, back_expand, 0)
    factors.append(send(gcoarse, sib_gcoarse, fsem.at[3], frsem.at[3], where["sibling"]))

    gc_rows = jnp.concatenate([gcoarse[n] for n in range(4)], axis=1)

    def back_merge(q, carry):
        rows = jnp.concatenate([gcoarse[n] for n in range(4)], axis=1)
        slab = w_merge[pl.ds(pl.multiple_of(q * 512, 512), 512), :]
        ghidden[q] = dot_nt(rows, slab).reshape(2, 64, 512)
        return carry

    lax.fori_loop(0, 4, back_merge, 0)
    gain = [gain_merge[:, q * 512 : (q + 1) * 512] for q in range(4)]
    first_sum = jnp.zeros((128, 1), f32)
    second_sum = jnp.zeros((128, 1), f32)
    for q in range(4):
        grad = ghidden[q].reshape(128, 512) * gain[q]
        first_sum += jnp.sum(grad, axis=-1, keepdims=True)
        second_sum += jnp.sum(grad * hat_m[:, q * 512 : (q + 1) * 512], axis=-1, keepdims=True)
    first_sum, second_sum = first_sum / 2048.0, second_sum / 2048.0
    rstd = rstd_m[:, 0:1]
    for q in range(4):
        grad = ghidden[q].reshape(128, 512) * gain[q]
        grad = rstd * (grad - first_sum - hat_m[:, q * 512 : (q + 1) * 512] * second_sum)
        grad = grad + c_patch[q].reshape(128, 512).astype(f32)
        ghidden[q] = grad.reshape(2, 64, 512)
        gbranch[q] = grad.astype(bf16).reshape(2, 64, 512)

    third = Exchange(where, gbranch, pack_patch, exchanges[2])
    third.begin()

    def store_at1(value):
        qkv_out[:, 0:1024] = value

    def store_at2(value):
        qkv_out[:, 1024:1536] = value[:, :512]
        proj_out[...] = value[:, 512:]

    def store_ex(value):
        ex_out[...] = value

    def store_mg(value):
        mg_out[...] = value

    streams = [
        Stream(where, acc_ex, "y", streams_scratch[0], store_ex),
        Stream(where, acc_mg, "x", streams_scratch[1], store_mg),
        Stream(where, acc_at1, "y", streams_scratch[2], store_at1),
        Stream(where, acc_at2, "x", streams_scratch[3], store_at2),
    ]
    for made in factors:
        made.wait_recv()

    def grad_expand(y, carry):
        left = jnp.concatenate((act[y, :, pl.ds(pl.multiple_of(core * 128, 128), 128)], sib_act[y]), axis=0).T
        for q in range(4):
            right = jnp.concatenate((c_patch[q].reshape(128, 512), sib_cot[q].reshape(128, 512)), axis=0)
            acc_ex[y, :, :, q * 512 : (q + 1) * 512] = dot(left, right).astype(bf16).reshape(4, 32, 512)
        return carry

    lax.fori_loop(0, 4, grad_expand, 0)
    streams[0].ring1.begin()

    def grad_merge(y, carry):
        left = jnp.concatenate(
            (merged[y, :, pl.ds(pl.multiple_of(core * 256, 256), 256)], sib_merged[y]), axis=0
        ).T
        for n in range(4):
            right = jnp.concatenate((gcoarse[n], sib_gcoarse[n]), axis=0)
            acc_mg[y, :, :, n * 256 : (n + 1) * 256] = dot(left, right).astype(bf16).reshape(4, 64, 256)
        return carry

    lax.fori_loop(0, 4, grad_merge, 0)
    streams[1].ring1.begin()

    third.arrive()
    for level in range(2):
        gbranch_w[:, level] = third.gather(level, to_window).astype(bf16).reshape(4, 64, 512)
    gattended[...] = dot_nt(gbranch_w[...].reshape(512, 512), w_proj[...]).astype(bf16).reshape(4, 128, 512)

    def attend_back(n, carry):
        w, g = n >> 2, n & 3
        queries, keys = head_stack(qkv[g, w]), qkv[4 + g, w]
        grads = head_stack(gattended[w, :, pl.ds(pl.multiple_of(g * 128, 128), 128)])
        grad_weights = dot_nt(grads, qkv[8 + g, w])
        weight = weights[w, g]
        wide = weight.astype(f32)
        delta = jnp.sum(wide * grad_weights, axis=-1, keepdims=True)
        grad_scores = (wide * (grad_weights - delta) * scale).astype(bf16)
        gqkv[g, w] = dot(head_row(grad_scores), head_stack(keys)).astype(bf16)
        gqkv[4 + g, w] = dot_tn(grad_scores, queries).astype(bf16)
        gqkv[8 + g, w] = dot_tn(weight, grads).astype(bf16)
        return carry

    lax.fori_loop(0, 16, attend_back, 0)
    streams[0].ring1.middle()
    streams[1].ring1.middle()

    def norm_back(half, carry):
        rows = jnp.concatenate([gqkv[n, pl.ds(2 * half, 2)].reshape(256, 128) for n in range(12)], axis=1)
        grad = dot_nt(rows, w_qkv[...]) * gain_attn
        hat = hat_w[pl.ds(2 * half, 2)].reshape(256, 512)
        rstd = rstd_w[pl.ds(2 * half, 2)].reshape(256, 128)[:, 0:1]
        first_mean = jnp.mean(grad, axis=-1, keepdims=True)
        second_mean = jnp.mean(grad * hat, axis=-1, keepdims=True)
        grad = rstd * (grad - first_mean - hat * second_mean)
        grolled[pl.ds(2 * half, 2)] = grad.astype(bf16).reshape(2, 2, 64, 512)
        return carry

    lax.fori_loop(0, 2, norm_back, 0)
    fourth = Exchange(where, grolled, pack_window, exchanges[3])
    fourth.begin()

    def grad_qkv(n, carry):
        right = jnp.concatenate([gqkv[2 * n + part].reshape(512, 128) for part in range(2)], axis=1)
        got = dot(normed_t[...], right).astype(bf16)
        at_source[:, :, :, :, pl.ds(pl.multiple_of(n * 256, 256), 256)] = got.reshape(4, 2, 4, 16, 256)
        return carry

    lax.fori_loop(0, 6, grad_qkv, 0)
    got = dot(attended_t[...], gbranch_w[...].reshape(512, 512)).astype(bf16)
    at_source[:, :, :, :, 1536:2048] = got.reshape(4, 2, 4, 16, 512)
    pair = send(at_source.at[:, 1 - core], got_at, asem.at[0], arsem.at[0], where["sibling"])
    streams[0].ring1.finish()
    streams[0].ring2.begin()
    streams[1].ring1.finish()
    streams[1].ring2.begin()

    pair.wait_recv()

    def sum_pair(n, carry):
        y, x = n // 4, lax.rem(n, 4)
        total = at_source[y, core, x].astype(f32) + got_at[y, x].astype(f32)
        acc_at1[y, x] = total[:, :1024].astype(bf16)
        acc_at2[y, x] = total[:, 1024:].astype(bf16)
        return carry

    lax.fori_loop(0, 16, sum_pair, 0)
    streams[2].ring1.begin()
    streams[3].ring1.begin()

    fine_hot = one_hot(fine_code(iota((256, 256), 0)) == patch_code(iota((1, 256), 1)))

    def expand(q, carry):
        rows = jnp.concatenate([act[n] for n in range(4)], axis=1)
        grown = dot(rows, w_expand[:, pl.ds(pl.multiple_of(q * 512, 512), 512)])
        out_patch[q] = (hidden[q].reshape(128, 512).astype(f32) + grown).astype(bf16).reshape(2, 64, 512)
        return carry

    lax.fori_loop(0, 4, expand, 0)
    for level in range(2):
        out_ref[level] = dot(fine_hot, out_patch[:, level].reshape(256, 512)).astype(bf16)

    streams[2].ring1.middle()
    streams[3].ring1.middle()
    fourth.arrive()
    for level in range(2):
        back = fourth.gather(level, to_patch).astype(bf16).astype(f32)
        total = (ghidden[:, level].reshape(256, 512) + back).astype(bf16)
        field_ref[level] = dot(fine_hot, total).astype(bf16)

    streams[0].ring2.middle()
    streams[1].ring2.middle()
    streams[2].ring1.finish()
    streams[2].ring2.begin()
    streams[3].ring1.finish()
    streams[3].ring2.begin()
    streams[0].ring2.finish()
    streams[0].z_begin()
    streams[1].ring2.finish()
    streams[1].z_begin()
    streams[2].ring2.middle()
    streams[3].ring2.middle()
    streams[2].ring2.finish()
    streams[2].z_begin()
    streams[3].ring2.finish()
    streams[3].z_begin()
    for stream in streams:
        stream.z_finish()

    for made in factors:
        made.wait_send()
    pair.wait_send()
    for each in (first, second, third, fourth):
        each.drain()
    for stream in streams:
        stream.drain()


def on_device(
    fine_field,
    cotangent,
    land_sea,
    shifts,
    gain_attn,
    w_qkv,
    w_proj,
    land_bias,
    gain_merge,
    w_merge,
    w_expand,
):
    vmem = pl.BlockSpec(memory_space=pltpu.VMEM)
    smem = pl.BlockSpec(memory_space=pltpu.SMEM)
    hbm = pl.BlockSpec(memory_space=pl.ANY)
    f32, bf16 = jnp.float32, jnp.bfloat16
    cells = (4, 2, 64, 512)
    scratch = [
        pltpu.VMEM((512, 1536), bf16),
        pltpu.VMEM((512, 512), bf16),
        pltpu.VMEM((2048, 1024), bf16),
        pltpu.VMEM((1024, 2048), bf16),
        pltpu.SemaphoreType.DMA((4,)),
        pltpu.VMEM((256, 640), bf16),
        pltpu.VMEM((256, 640), bf16),
        pltpu.VMEM((64, 256), bf16),
        pltpu.VMEM((64, 256), bf16),
        pltpu.VMEM(cells, bf16),
        pltpu.VMEM(cells, bf16),
        pltpu.VMEM(cells, bf16),
        pltpu.VMEM(cells, f32),
        pltpu.VMEM((4, 2, 64, 128), f32),
        pltpu.VMEM((12, 4, 128, 128), bf16),
        pltpu.VMEM((4, 4, 512, 128), bf16),
        pltpu.VMEM((4, 128, 512), bf16),
        pltpu.VMEM(cells, bf16),
        pltpu.VMEM(cells, bf16),
        pltpu.VMEM((128, 2048), f32),
        pltpu.VMEM((128, 128), f32),
        pltpu.VMEM((4, 128, 512), bf16),
        pltpu.VMEM((4, 128, 256), f32),
        pltpu.VMEM((4, 128, 256), bf16),
        pltpu.VMEM((4, 128, 256), bf16),
        pltpu.VMEM(cells, bf16),
        pltpu.VMEM(cells, f32),
        pltpu.VMEM(cells, bf16),
        pltpu.VMEM(cells, bf16),
        pltpu.VMEM((4, 128, 128), bf16),
        pltpu.VMEM((4, 128, 256), bf16),
        pltpu.VMEM((4, 128, 256), bf16),
        pltpu.SemaphoreType.DMA((4,)),
        pltpu.SemaphoreType.DMA((4,)),
        pltpu.VMEM(cells, bf16),
        pltpu.VMEM((4, 128, 512), bf16),
        pltpu.VMEM((12, 4, 128, 128), bf16),
        pltpu.VMEM(cells, bf16),
        pltpu.VMEM((512, 512), bf16),
        pltpu.VMEM((512, 512), bf16),
        pltpu.VMEM((4, 2, 4, 16, 2048), bf16),
        pltpu.VMEM((4, 4, 16, 1024), bf16),
        pltpu.VMEM((4, 4, 16, 1024), bf16),
        pltpu.VMEM((4, 4, 32, 2048), bf16),
        pltpu.VMEM((4, 4, 64, 1024), bf16),
        pltpu.VMEM((4, 4, 16, 2048), bf16),
        pltpu.SemaphoreType.DMA((1,)),
        pltpu.SemaphoreType.DMA((1,)),
    ]
    for _ in range(4):
        scratch += exchange_scratch()
    scratch += stream_scratch(32, 2048, bf16)
    scratch += stream_scratch(64, 1024, bf16)
    scratch += stream_scratch(16, 1024, f32)
    scratch += stream_scratch(16, 1024, f32)
    scratch += [pltpu.VMEM((4, 1, 128), f32)]
    results = pl.pallas_call(
        block_kernel,
        out_shape=(
            jax.ShapeDtypeStruct((2, 256, 512), bf16),
            jax.ShapeDtypeStruct((2, 256, 512), bf16),
            jax.ShapeDtypeStruct((8, 1536), f32),
            jax.ShapeDtypeStruct((8, 512), f32),
            jax.ShapeDtypeStruct((32, 1024), f32),
            jax.ShapeDtypeStruct((16, 2048), f32),
        ),
        in_specs=[smem, smem] + [vmem] * 5 + [hbm] * 4,
        out_specs=(vmem,) * 6,
        scratch_shapes=scratch,
        compiler_params=pltpu.CompilerParams(
            collective_id=0, has_side_effects=True, vmem_limit_bytes=60 * 2**20
        ),
        name="attention_block",
    )(
        shifts,
        land_bias,
        fine_field.reshape(2, 256, 512),
        cotangent.reshape(2, 256, 512),
        land_sea,
        gain_attn.reshape(1, 512),
        gain_merge.reshape(1, 2048),
        w_qkv,
        w_proj,
        w_merge,
        w_expand,
    )
    output, grad_field = results[0].reshape(2, 8, 32, 512), results[1].reshape(2, 8, 32, 512)
    return (output, grad_field) + tuple(results[2:])


def solution(mesh):
    return jax.shard_map(
        on_device,
        mesh=mesh,
        in_specs=(
            P("rep", "lat", "lon", None),
            P("rep", "lat", "lon", None),
            P(),
            P(),
            P(),
            P(),
            P(),
            P(),
            P(),
            P(),
            P(),
        ),
        out_specs=(
            P("rep", "lat", "lon", None),
            P("rep", "lat", "lon", None),
            P(("rep", "lat", "lon"), None),
            P(("rep", "lat", "lon"), None),
            P(("rep", "lat", "lon"), None),
            P(("rep", "lat", "lon"), None),
        ),
        check_vma=False,
    )
```

time: 262 us -> 101 us (0.39); the launches traced: 258 us -> 99.5 us
  local copies, waits for them, and re-layouts: 105 us -> 9.64 us
  matrix products: 37.1 us -> 0 us
  Pallas kernels: 54 us -> 89.2 us
  other arithmetic: 22.3 us -> 0 us
  starting transfers between devices: 14.2 us -> 0 us
  waiting for transfers between devices: 13.6 us -> 0 us
  between operations: 11.3 us -> 0.65 us
    dot_general x18 -> x0, matrix products: 37.1 us -> none  [the longest x3 6.78 us: window_core(): jnp.einsum('whqk,wkhd->wqhd', weights.astype(jnp.float32), window_values....]
    pallas_call x1, Pallas kernels: 54 us -> 89.2 us  [on_device(): pl.pallas_call(block_kernel, out_shape=(jax.ShapeDtypeStruct((2, 256, 512...]
    another operation x7 -> x0, local copies, waits for them, and re-layouts: 32.8 us -> none  [the longest x2 13.4 us: from_windows(): array.reshape(row_count // window, col_count // window, levels, window, w...]
    reshape x7 -> x0, local copies, waits for them, and re-layouts: 16.6 us -> none  [the longest x2 6.18 us: unarrange(): flat.reshape(levels, row_count // 2, col_count // 2, 2, 2, channels)]
    ppermute x8 -> x0, starting transfers between devices: 14.2 us -> none  [from_behind(): return lax.ppermute(value, axis, pairs)]
    ppermute x8 -> x0, waiting for transfers between devices: 13.6 us -> none  [from_behind(): return lax.ppermute(value, axis, pairs)]
    unnamed x75 -> x6, local copies, waits for them, and re-layouts: 22.7 us -> 9.64 us
    transpose x8 -> x0, local copies, waits for them, and re-layouts: 11 us -> none  [the longest x2 5.41 us: unarrange(): shaped.transpose(0, 1, 3, 2, 4, 5)]
  transfers between devices with their start and end apart: 8 -> 0, of which waited for: 4 -> 0; matrix products, arithmetic and copies ran while one was open for 15% -> 0% of each run, Pallas kernels for 21% -> 0%
where the time goes in v2:
time: 101 us; the launch traced here: 99.5 us
  Pallas kernels  89.2 us (88%)
  local copies, waits for them, and re-layouts  9.64 us (10%)
    pallas_call x1, Pallas kernels, on_device(): pl.pallas_call(block_kernel, out_shape=(jax.ShapeDtypeStruct((2, 256, 512...  89.2 us
    unnamed x6, local copies, waits for them, and re-layouts  9.64 us

profile of v2, /device:TPU:1, one launch (start us, length us, event | category | flops | bytes accessed | tf_op | source)
XLA Modules:
  0.0 99.5 jit_solution(2123291904153188500)
XLA Ops:
  0.6 89.2 %attention_block.1 = (bf16[2,256,512]{2,1,0:T(8,128)(2,1)}, bf16[2,256,512]{2,1,0:T(8,128)(2,1)}, f32[8,1536]{1,0:T(8,128)}, f32[8,512]{1,0:T(8,128)}, f32[32,1024]{1,0:T(8,128)}, /*index=5*/f32[16,2048]{1,0:T(8,128)}) custom-call(s32[2]{0:T(128)} %shifts_ref.1, f32[16]{0:T(128)} %bias_ref.1, bf16[2,256,512]{2,1,0:T(8,128)(2,1)} %bitcast.6, ...), custom_call_target="tpu_custom_call" | custom-call | tf_op jit(solution)/shard_map/attention_block/pallas_call | solution.py:795
  89.9 1.9 %copy.23 = bf16[2,8,32,512]{3,2,1,0:T(8,128)(2,1)} copy(bf16[2,8,32,512]{3,2,1,0:T(8,128)(2,1)} %bitcast.9) | data formatting | bytes 1048576
  91.8 1.9 %copy.24 = bf16[2,8,32,512]{3,2,1,0:T(8,128)(2,1)} copy(bf16[2,8,32,512]{3,2,1,0:T(8,128)(2,1)} %bitcast.8) | data formatting | bytes 1048576
  93.6 1.4 %copy.25 = f32[8,1536]{1,0:T(8,128)} copy(f32[8,1536]{1,0:T(8,128)} %get-tuple-element.26) | data formatting | bytes 98304
  95.1 1.3 %copy.26 = f32[8,512]{1,0:T(8,128)} copy(f32[8,512]{1,0:T(8,128)} %get-tuple-element.27) | data formatting | bytes 32768
  96.4 1.6 %copy.27 = f32[32,1024]{1,0:T(8,128)} copy(f32[32,1024]{1,0:T(8,128)} %get-tuple-element.28) | data formatting | bytes 262144
  98.0 1.6 %copy.28 = f32[16,2048]{1,0:T(8,128)} copy(f32[16,2048]{1,0:T(8,128)} %get-tuple-element.29) | data formatting | bytes 262144

commit v3 on v2

v3 whole, which is shorter than its diff:
```python
import functools

import jax
import jax.numpy as jnp
from jax import lax
from jax.experimental import pallas as pl
from jax.experimental.pallas import tpu as pltpu
from jax.sharding import PartitionSpec as P

epsilon = 1e-05

MESH = pl.DeviceIdType.MESH


class Ring:
    def __init__(self, place, right, left, block, store, bufs, send_sems, recv_sems, half):
        self.place, self.right, self.left = place, right, left
        self.block, self.store = block, store
        self.bufs, self.outs = bufs[0], bufs[1]
        self.send_sems, self.recv_sems = send_sems, recv_sems
        self.half = half
        self.copies = {}

    def part(self, k, which):
        return self.block(k).at[:, :, pl.ds(which * self.half, self.half)]

    def copy(self, slot, source, target):
        made = pltpu.make_async_remote_copy(
            src_ref=source,
            dst_ref=self.bufs.at[slot],
            send_sem=self.send_sems.at[slot],
            recv_sem=self.recv_sems.at[slot],
            device_id=target,
            device_id_type=MESH,
        )
        made.start()
        self.copies[slot] = made

    def begin(self):
        ahead = lax.rem(self.place + 1, 4)
        across = lax.rem(self.place + 2, 4)
        behind = lax.rem(self.place + 3, 4)
        self.copy(0, self.part(across, 0), self.right)
        self.copy(3, self.part(across, 1), self.left)
        self.copy(1, self.part(ahead, 1), self.right)
        self.copy(4, self.part(behind, 0), self.left)

    def middle(self):
        ahead = lax.rem(self.place + 1, 4)
        behind = lax.rem(self.place + 3, 4)
        for slot, which, k, out, target in ((0, 0, ahead, 0, self.right), (3, 1, behind, 1, self.left)):
            self.copies[slot].wait_recv()

            def add(i, carry, slot=slot, which=which, k=k, out=out):
                mine = self.block(k)[i, :, pl.ds(which * self.half, self.half)]
                total = mine.astype(jnp.float32) + self.bufs[slot, i].astype(jnp.float32)
                self.outs[out, i] = total.astype(jnp.bfloat16)
                return carry

            lax.fori_loop(0, 4, add, 0)
            self.copy(2 if out == 0 else 5, self.outs.at[out], target)

    def finish(self):
        for slot in (1, 2, 4, 5):
            self.copies[slot].wait_recv()

        def add(i, carry):
            totals = []
            for which, first, second in ((0, 2, 4), (1, 5, 1)):
                mine = self.block(self.place)[i, :, pl.ds(which * self.half, self.half)]
                totals.append(
                    mine.astype(jnp.float32)
                    + self.bufs[first, i].astype(jnp.float32)
                    + self.bufs[second, i].astype(jnp.float32)
                )
            self.store(i, totals[0], totals[1])
            return carry

        lax.fori_loop(0, 4, add, 0)

    def drain(self):
        for slot in range(6):
            self.copies[slot].wait_send()


class Stream:
    def __init__(self, where, source, first_axis, paired, scratch, store):
        buf, out, red, got, ssem, rsem = scratch
        self.where, self.paired, self.store = where, paired, store
        self.red, self.got, self.ssem, self.rsem = red, got, ssem, rsem
        self.half = source.shape[3] // 2
        axes = {
            "y": (where["y"], where["up"], where["down"], lambda k: source.at[k]),
            "x": (where["x"], where["east"], where["west"], lambda k: source.at[:, k]),
        }
        self.second_axis = "x" if first_axis == "y" else "y"
        place, right, left, block = axes[first_axis]
        self.ring = Ring(place, right, left, block, self.keep, (buf, out), ssem, rsem, self.half)
        self.place = where[self.second_axis]

    def keep(self, i, first, second):
        if self.paired:
            for z in range(2):
                rows = slice(z * 8, z * 8 + 8)
                both = jnp.concatenate((first[rows], second[rows]), axis=0)
                self.red[i, z] = both.astype(jnp.bfloat16)
        else:
            self.red[i] = jnp.concatenate((first, second), axis=1).astype(jnp.bfloat16)

    def spread(self):
        where = self.where
        self.copies = []
        for n in range(1, 8 if self.paired else 4):
            d, e = (n // 2, n % 2) if self.paired else (n, 0)
            k = lax.rem(self.place + d, 4)
            block = self.red.at[k, where["z"] * (1 - e) + (1 - where["z"]) * e] if self.paired else self.red.at[k]
            if self.second_axis == "x":
                lon = lax.rem(where["lon"] + 2 * d, 8)
                target = {"lon": lon + e * (1 - 2 * where["z"])}
            else:
                target = {
                    "lat": lax.rem(where["lat"] + 2 * d, 8),
                    "lon": where["lon"] + e * (1 - 2 * where["z"]),
                }
            made = pltpu.make_async_remote_copy(
                src_ref=block,
                dst_ref=self.got.at[n - 1],
                send_sem=self.ssem.at[5 + n],
                recv_sem=self.rsem.at[5 + n],
                device_id=target,
                device_id_type=MESH,
            )
            made.start()
            self.copies.append(made)

    def end(self):
        for made in self.copies:
            made.wait_recv()
        mine = self.red[self.place, self.where["z"]] if self.paired else self.red[self.place]
        total = mine.astype(jnp.float32)
        for n in range(len(self.copies)):
            total += self.got[n].astype(jnp.float32)
        if self.paired:
            total = jnp.concatenate((total[:8], total[8:]), axis=1)
        self.store(total)

    def drain(self):
        self.ring.drain()
        for made in self.copies:
            made.wait_send()


def stream_scratch(rows, width, paired):
    half, bf16 = width // 2, jnp.bfloat16
    return [
        pltpu.VMEM((6, 4, rows, half), bf16),
        pltpu.VMEM((2, 4, rows, half), bf16),
        pltpu.VMEM((4, 2, 16, half) if paired else (4, rows, width), bf16),
        pltpu.VMEM((7, 16, half) if paired else (3, rows, width), bf16),
        pltpu.SemaphoreType.DMA((13,)),
        pltpu.SemaphoreType.DMA((13,)),
    ]


def places():
    lat, lon = lax.axis_index("lat"), lax.axis_index("lon")
    core, z = lax.rem(lat, 2), lax.rem(lon, 2)
    return {
        "lat": lat,
        "lon": lon,
        "y": lat // 2,
        "x": lon // 2,
        "core": core,
        "z": z,
        "up": {"lat": lax.rem(lat + 2, 8)},
        "down": {"lat": lax.rem(lat + 6, 8)},
        "east": {"lon": lax.rem(lon + 2, 8)},
        "west": {"lon": lax.rem(lon + 6, 8)},
        "beside": {"lon": lon + 1 - 2 * z},
        "sibling": {"lat": lat + 1 - 2 * core},
        "corner": {"lat": lat + 1 - 2 * core, "lon": lon + 1 - 2 * z},
    }


def dot(a, b):
    return lax.dot_general(a, b, (((1,), (0,)), ((), ())), preferred_element_type=jnp.float32)


def dot_nt(a, b):
    return lax.dot_general(a, b, (((1,), (1,)), ((), ())), preferred_element_type=jnp.float32)


def dot_tn(a, b):
    return lax.dot_general(a, b, (((0,), (0,)), ((), ())), preferred_element_type=jnp.float32)


def code_of(row, col):
    return (row + 16) * 64 + (col + 16)


def fine_code(s):
    return code_of(s >> 5, s & 31)


def patch_code(s):
    quarter, coarse = s >> 6, s & 63
    return code_of(2 * (coarse >> 4) + (quarter >> 1), 2 * (coarse & 15) + (quarter & 1))


def window_code(s):
    return code_of((s & 63) >> 3, 8 * (s >> 6) + (s & 7))


def rim_code(t):
    kind, c4 = t >> 5, t & 3
    row = jnp.where(kind < 2, (t & 31) >> 2, ((t & 15) >> 2) + jnp.where(kind == 2, 8, -4))
    west = jnp.where(kind < 2, kind & 1, (t >> 4) & 1)
    return code_of(row, c4 + 32 - 36 * west)


def iota(shape, axis):
    return lax.broadcasted_iota(jnp.int32, shape, axis)


def one_hot(same):
    return jnp.where(same, 1.0, 0.0).astype(jnp.bfloat16)


def fill_gather(ref, target_code, source_code, offset):
    target = target_code(iota((256, 128), 0)) + offset
    lane = iota((1, 128), 1)
    half = (lane >> 5 << 6) + (lane & 31)
    pieces = (
        source_code(lane),
        source_code(lane + 128),
        source_code(half + 32) - 8 * 64,
        source_code(half) + 8 * 64,
        rim_code(lane),
    )
    for n, piece in enumerate(pieces):
        ref[:, n * 128 : (n + 1) * 128] = one_hot(target == piece)


def fill_pack(ref, source_code):
    t = iota((64, 256), 0)
    target = code_of((t & 31) >> 2, (t & 3) + jnp.where(t >= 32, 28, 0))
    ref[...] = one_hot(target == source_code(iota((1, 256), 1)))


class Exchange:
    def __init__(self, where, source, pack, scratch):
        self.where, self.source, self.pack = where, source, pack
        self.packed, self.north, self.south, self.rim, self.ssem, self.rsem = scratch
        self.copies = []

    def make(self, n, source, target, lat, lon):
        return pltpu.make_async_remote_copy(
            src_ref=source,
            dst_ref=target,
            send_sem=self.ssem.at[n],
            recv_sem=self.rsem.at[n],
            device_id={
                "lat": lax.rem(self.where["lat"] + lat + 8, 8),
                "lon": lax.rem(self.where["lon"] + lon + 8, 8),
            },
            device_id_type=MESH,
        )

    def rows(self, quarter):
        first, last = pl.ds(0, 32), pl.ds(32, 32)
        return (
            self.make(quarter, self.source.at[quarter, :, first], self.south.at[quarter], -1, 0),
            self.make(quarter + 4, self.source.at[quarter, :, last], self.north.at[quarter], 1, 0),
        )

    def begin_rows(self, quarter):
        for made in self.rows(quarter):
            made.start()

    def begin_rim(self, quarters=(0, 1, 2, 3)):
        moves = jnp.concatenate([self.pack[:, q * 64 : (q + 1) * 64] for q in quarters], axis=1)
        for level in range(2):
            cells = jnp.concatenate([self.source[q, level] for q in quarters], axis=0)
            rim = dot(moves, cells).astype(jnp.bfloat16)
            self.packed[0, level] = rim[:32]
            self.packed[1, level] = rim[32:]
        near, far = pl.ds(0, 16), pl.ds(16, 16)
        packed, rim = self.packed, self.rim
        self.copies = [
            self.make(8, packed.at[0], rim.at[:, pl.ds(0, 32)], 0, -1),
            self.make(9, packed.at[1], rim.at[:, pl.ds(32, 32)], 0, 1),
            self.make(10, packed.at[0, :, near], rim.at[:, pl.ds(64, 16)], -1, -1),
            self.make(11, packed.at[1, :, near], rim.at[:, pl.ds(80, 16)], -1, 1),
            self.make(12, packed.at[0, :, far], rim.at[:, pl.ds(96, 16)], 1, -1),
            self.make(13, packed.at[1, :, far], rim.at[:, pl.ds(112, 16)], 1, 1),
        ]
        for made in self.copies:
            made.start()

    def begin(self):
        for quarter in range(4):
            self.begin_rows(quarter)
        self.begin_rim()

    def arrive(self):
        for quarter in range(4):
            self.copies += self.rows(quarter)
        for made in self.copies:
            made.wait_recv()

    def gather(self, level, moves):
        cells = jnp.concatenate(
            (
                self.source[:, level].reshape(256, 512),
                self.north[:, level].reshape(128, 512),
                self.south[:, level].reshape(128, 512),
                self.rim[level],
            ),
            axis=0,
        )
        return dot(moves[...], cells)

    def drain(self):
        for made in self.copies:
            made.wait_send()


def exchange_scratch():
    bf16 = jnp.bfloat16
    return [
        pltpu.VMEM((2, 2, 32, 512), bf16),
        pltpu.VMEM((4, 2, 32, 512), bf16),
        pltpu.VMEM((4, 2, 32, 512), bf16),
        pltpu.VMEM((2, 128, 512), bf16),
        pltpu.SemaphoreType.DMA((14,)),
        pltpu.SemaphoreType.DMA((14,)),
    ]


def send(source, target, ssem, rsem, device):
    made = pltpu.make_async_remote_copy(
        src_ref=source, dst_ref=target, send_sem=ssem, recv_sem=rsem, device_id=device, device_id_type=MESH
    )
    made.start()
    return made


def block_kernel(
    shifts_ref,
    bias_ref,
    fine_ref,
    cot_ref,
    land_ref,
    gain_attn_ref,
    gain_merge_ref,
    w_qkv_hbm,
    w_proj_hbm,
    w_merge_hbm,
    w_expand_hbm,
    out_ref,
    field_ref,
    qkv_out,
    proj_out,
    mg_out,
    ex_out,
    *scratch,
):
    scratch = list(scratch)

    def take(n):
        got = scratch[:n]
        del scratch[:n]
        return got

    f32, bf16 = jnp.float32, jnp.bfloat16
    w_qkv, w_proj, w_merge, w_expand, wsem = take(5)
    to_window, to_patch, pack_patch, pack_window = take(4)
    x_patch, c_patch, normed_w, hat_w, rstd_w = take(5)
    qkv, qkv_t, weights, branch = take(4)
    hidden, hat_m, rstd_m, merged, slope, act, gcoarse, out_patch, ghidden, gbranch = take(10)
    cots, gcoarses, act_t, merged_t, acts, mergeds, fsem, frsem = take(8)
    gbranch_w, gattended, gattended_t, gqkv, grolled, normed_t, attended_t = take(7)
    sib_normed, sib_attended, sib_gbranch, sib_gqkv, asem, arsem = take(6)
    acc_ex, acc_mg, acc_pj, acc_q1, acc_q2 = take(5)
    exchanges = [take(6) for _ in range(4)]
    streams_scratch = [take(6) for _ in range(5)]

    where = places()
    core, lat, lon = where["core"], where["lat"], where["lon"]
    loads = []
    for n, (far, near) in enumerate(
        ((w_qkv_hbm, w_qkv), (w_proj_hbm, w_proj), (w_merge_hbm, w_merge), (w_expand_hbm, w_expand))
    ):
        made = pltpu.make_async_copy(far, near, wsem.at[n])
        made.start()
        loads.append(made)

    barrier = pltpu.get_barrier_semaphore()
    beside = lon + 1 - 2 * where["z"]
    around = [(lat + a, lon + b) for a in (7, 8, 9) for b in (7, 8, 9) if (a, b) != (8, 8)]
    around += [(lat, lon + b) for b in range(2, 7)] + [(lat + a, lon) for a in (2, 4, 6)]
    around += [(lat + a, beside) for a in (2, 4, 6)]
    for a, b in around:
        pl.semaphore_signal(
            barrier, inc=1, device_id={"lat": lax.rem(a, 8), "lon": lax.rem(b, 8)}, device_id_type=MESH
        )

    shift_lat, shift_lon = shifts_ref[0], shifts_ref[1]
    low_lat = shift_lat <= 4
    off_lat = jnp.where(low_lat, shift_lat, shift_lat - 8)
    off_lon = jnp.where(shift_lon <= 4, shift_lon, shift_lon - 8)
    offset = off_lat * 64 + off_lon

    fill_pack(pack_patch, patch_code)
    arrange_hot = one_hot(patch_code(iota((256, 256), 0)) == fine_code(iota((1, 256), 1)))
    for source, target in ((fine_ref, x_patch), (cot_ref, c_patch)):
        for level in range(2):
            target[:, level] = dot(arrange_hot, source[level]).astype(bf16).reshape(4, 64, 512)
    pl.semaphore_wait(barrier, len(around))

    first = Exchange(where, x_patch, pack_patch, exchanges[0])
    first.begin()
    sent = []

    def share(n, source, target, name):
        made = send(source, target, fsem.at[n], frsem.at[n], where[name])
        sent.append(made)
        return made

    cot_side = share(0, c_patch, cots.at[0], "sibling")
    cot_beside = share(1, c_patch, cots.at[1], "beside")

    fill_gather(to_window, window_code, patch_code, offset)
    fill_gather(to_patch, patch_code, window_code, -offset)
    fill_pack(pack_window, window_code)

    (land_keys,) = take(1)

    def land_window(w, carry):
        key = iota((128, 256), 0)
        col_at = (32 * lon + off_lon + 8 * w + (key & 7) + 256) & 255
        land_rows = dot_nt(one_hot(iota((128, 256), 1) == col_at), land_ref[...].astype(bf16))
        row_at = (8 * lat + off_lat + ((iota((128, 64), 0) & 63) >> 3) + 64) & 63
        land = jnp.sum(jnp.where(iota((128, 64), 1) == row_at, land_rows, 0.0), axis=1, keepdims=True)
        land_keys[w] = jnp.broadcast_to(land, (128, 128))
        return carry

    lax.fori_loop(0, 4, land_window, 0)

    band = jnp.where(low_lat, lat, lax.rem(lat + 7, 8))

    def region(cell):
        row = 8 * band + ((cell & 63) >> 3)
        return jnp.where(row >= 56, 1, 0) + jnp.where(row >= 64 - shift_lat, 1, 0)

    same_region = region(iota((128, 128), 0)) == region(iota((128, 128), 1))
    heads = [jnp.where(iota((1, 128), 1) >> 5 == h, 1.0, 0.0).astype(bf16) for h in range(4)]

    def head_stack(value):
        return jnp.concatenate([value * head for head in heads], axis=0)

    def head_blocks(value):
        blocks = []
        for h in range(4):
            pieces = [value[32 * h : 32 * h + 32]]
            if h > 0:
                pieces.insert(0, jnp.zeros((32 * h, 128), bf16))
            if h < 3:
                pieces.append(jnp.zeros((96 - 32 * h, 128), bf16))
            blocks.append(jnp.concatenate(pieces, axis=0))
        return jnp.concatenate(blocks, axis=1)

    def under(value):
        return jnp.concatenate([value[:, h * 128 : (h + 1) * 128] for h in range(4)], axis=0)

    gain_attn = gain_attn_ref[...]
    first.arrive()
    for level in range(2):
        cells = first.gather(level, to_window)
        average = jnp.mean(cells, axis=-1, keepdims=True)
        centred = cells - average
        rstd = lax.rsqrt(jnp.mean(centred * centred, axis=-1, keepdims=True) + epsilon)
        hat = centred * rstd
        hat_w[:, level] = hat.reshape(4, 64, 512)
        rstd_w[:, level] = jnp.broadcast_to(rstd, (256, 128)).reshape(4, 64, 128)
        normed_w[:, level] = (hat * gain_attn).astype(bf16).reshape(4, 64, 512)

    loads[0].wait()
    normed = normed_w[...].reshape(512, 512)

    def project(n, carry):
        cols = w_qkv[:, pl.ds(pl.multiple_of(n * 256, 256), 256)]
        got = dot(normed_w[...].reshape(512, 512), cols).astype(bf16)
        for part in range(2):
            piece = got[:, part * 128 : (part + 1) * 128]
            qkv[2 * n + part] = piece.reshape(4, 128, 128)
            turned = piece.T
            for w in range(4):
                qkv_t[2 * n + part, w] = turned[:, w * 128 : (w + 1) * 128]
        return carry

    lax.fori_loop(0, 6, project, 0)
    normed_t[...] = normed.T.reshape(4, 2, 64, 512)
    pairs = [send(normed_t.at[:, 1 - core], sib_normed, asem.at[0], arsem.at[0], where["sibling"])]

    scale = 32.0 ** (-0.5)

    def attend(w, g):
        scores = dot(qkv[4 + g, w], head_blocks(qkv_t[g, w]))
        parts = []
        for h in range(4):
            score = scores[:, h * 128 : (h + 1) * 128] * scale + bias_ref[4 * g + h] * land_keys[w]
            score = jnp.where(same_region, score, -1000000000.0)
            raised = jnp.exp(score - jnp.max(score, axis=0, keepdims=True))
            parts.append((raised * (1.0 / jnp.sum(raised, axis=0, keepdims=True))).astype(bf16))
        weights[w, g] = jnp.concatenate(parts, axis=1)
        mixed = dot(head_blocks(qkv_t[8 + g, w]), jnp.concatenate(parts, axis=0))
        attended_t[g, :, :, pl.ds(pl.multiple_of(w * 128, 128), 128)] = mixed.astype(bf16).reshape(2, 64, 128)

    second = Exchange(where, branch, pack_window, exchanges[1])

    def attend_window(n, carry):
        w = lax.rem(3 * n, 4)
        for g in range(4):
            attend(w, g)
        mixed = attended_t[:, :, :, pl.ds(pl.multiple_of(w * 128, 128), 128)].reshape(512, 128).T
        branch[w] = dot(mixed, w_proj[...]).astype(bf16).reshape(2, 64, 512)
        second.begin_rows(w)
        return carry

    loads[1].wait()
    lax.fori_loop(0, 2, attend_window, 0)
    second.begin_rim((0, 3))
    lax.fori_loop(2, 4, attend_window, 0)
    pairs.append(send(attended_t.at[:, 1 - core], sib_attended, asem.at[1], arsem.at[1], where["sibling"]))
    cot_beside.wait_recv()
    cot_corner = share(2, cots.at[1], cots.at[2], "sibling")
    second.arrive()
    for level in range(2):
        back = second.gather(level, to_patch).reshape(4, 64, 512)
        hidden[:, level] = (x_patch[:, level].astype(f32) + back.astype(bf16).astype(f32)).astype(bf16)

    def patches(ref):
        return jnp.concatenate([ref[q].reshape(128, 512) for q in range(4)], axis=1)

    gain_merge = gain_merge_ref[...]
    cells = patches(hidden).astype(f32)
    average = jnp.mean(cells, axis=-1, keepdims=True)
    centred = cells - average
    rstd = lax.rsqrt(jnp.mean(centred * centred, axis=-1, keepdims=True) + epsilon)
    hat = centred * rstd
    hat_m[...] = hat
    rstd_m[...] = jnp.broadcast_to(rstd, (128, 128))
    scaled = (hat * gain_merge).astype(bf16)
    for q in range(4):
        merged[q] = scaled[:, q * 512 : (q + 1) * 512]

    def part_rows(target, y, value, deep):
        value = value.T.reshape(2, 4, 2, deep, 128)
        for c in range(2):
            for z in range(2):
                target[c, z, y] = value[c, :, z]

    for q in range(4):
        part_rows(merged_t, q, scaled[:, q * 512 : (q + 1) * 512], 32)
    side, level_z = 1 - core, where["z"]
    merged_parts = [
        share(3, merged_t.at[side, level_z], mergeds.at[0], "sibling"),
        share(4, merged_t.at[core, 1 - level_z], mergeds.at[1], "beside"),
        share(5, merged_t.at[side, 1 - level_z], mergeds.at[2], "corner"),
    ]

    loads[2].wait()
    bend = 0.7978845608028654

    def merge(n, carry):
        rows = jnp.concatenate([merged[q] for q in range(4)], axis=1)
        coarse = dot(rows, w_merge[:, pl.ds(pl.multiple_of(n * 256, 256), 256)])
        square = coarse * coarse
        bent = jnp.tanh(bend * (coarse + 0.044715 * (coarse * square)))
        active = (0.5 * coarse * (1.0 + bent)).astype(bf16)
        act[n] = active
        part_rows(act_t, n, active, 16)
        inner = bend * (1.0 + 3.0 * 0.044715 * square)
        slope[n] = 0.5 * (1.0 + bent) + 0.5 * coarse * (1.0 - bent * bent) * inner
        return carry

    lax.fori_loop(0, 4, merge, 0)
    act_parts = [
        share(6, act_t.at[side, level_z], acts.at[0], "sibling"),
        share(7, act_t.at[core, 1 - level_z], acts.at[1], "beside"),
        share(8, act_t.at[side, 1 - level_z], acts.at[2], "corner"),
    ]

    loads[3].wait()

    def back_expand(n, carry):
        rows = patches(c_patch)
        slab = w_expand[pl.ds(pl.multiple_of(n * 256, 256), 256), :]
        gcoarse[n] = (slope[n] * dot_nt(rows, slab)).astype(bf16)
        return carry

    lax.fori_loop(0, 4, back_expand, 0)
    gcoarse_side = share(9, gcoarse, gcoarses.at[0], "sibling")
    gcoarse_beside = share(10, gcoarse, gcoarses.at[1], "beside")

    def store_q1(value):
        qkv_out[:, 0:768] = value

    def store_q2(value):
        qkv_out[:, 768:1536] = value

    def store_pj(value):
        proj_out[...] = value

    def store_ex(value):
        ex_out[...] = value

    def store_mg(value):
        mg_out[...] = value

    stream_ex = Stream(where, acc_ex, "x", False, streams_scratch[0], store_ex)
    stream_mg = Stream(where, acc_mg, "y", False, streams_scratch[1], store_mg)
    stream_pj = Stream(where, acc_pj, "x", True, streams_scratch[2], store_pj)
    stream_q1 = Stream(where, acc_q1, "y", True, streams_scratch[3], store_q1)
    stream_q2 = Stream(where, acc_q2, "x", True, streams_scratch[4], store_q2)
    for made in act_parts:
        made.wait_recv()
    cot_side.wait_recv()
    cot_corner.wait_recv()

    def grad_expand(q, carry):
        parts = [act_t[core, level_z]] + [acts[n] for n in range(3)]
        left = jnp.concatenate([part.reshape(256, 128) for part in parts], axis=1)
        parts = [c_patch[q]] + [cots[n, q] for n in range(3)]
        right = jnp.concatenate([part.reshape(128, 512) for part in parts], axis=0)
        got = dot(left, right).astype(bf16).reshape(4, 4, 16, 512)
        acc_ex[:, :, :, pl.ds(pl.multiple_of(q * 512, 512), 512)] = got
        return carry

    lax.fori_loop(0, 4, grad_expand, 0)
    stream_ex.ring.begin()

    def back_merge(q, carry):
        rows = jnp.concatenate([gcoarse[n] for n in range(4)], axis=1)
        slab = w_merge[pl.ds(pl.multiple_of(q * 512, 512), 512), :]
        ghidden[q] = dot_nt(rows, slab).reshape(2, 64, 512)
        return carry

    lax.fori_loop(0, 4, back_merge, 0)
    gain = [gain_merge[:, q * 512 : (q + 1) * 512] for q in range(4)]
    first_sum = jnp.zeros((128, 1), f32)
    second_sum = jnp.zeros((128, 1), f32)
    for q in range(4):
        grad = ghidden[q].reshape(128, 512) * gain[q]
        first_sum += jnp.sum(grad, axis=-1, keepdims=True)
        second_sum += jnp.sum(grad * hat_m[:, q * 512 : (q + 1) * 512], axis=-1, keepdims=True)
    first_sum, second_sum = first_sum / 2048.0, second_sum / 2048.0
    rstd = rstd_m[:, 0:1]
    for q in range(4):
        grad = ghidden[q].reshape(128, 512) * gain[q]
        grad = rstd * (grad - first_sum - hat_m[:, q * 512 : (q + 1) * 512] * second_sum)
        grad = grad + c_patch[q].reshape(128, 512).astype(f32)
        ghidden[q] = grad.reshape(2, 64, 512)
        gbranch[q] = grad.astype(bf16).reshape(2, 64, 512)

    third = Exchange(where, gbranch, pack_patch, exchanges[2])
    third.begin()

    gcoarse_beside.wait_recv()
    gcoarse_corner = share(11, gcoarses.at[1], gcoarses.at[2], "sibling")
    for made in merged_parts:
        made.wait_recv()
    gcoarse_side.wait_recv()
    gcoarse_corner.wait_recv()

    def grad_merge(n, carry):
        parts = [merged_t[core, level_z]] + [mergeds[k] for k in range(3)]
        left = jnp.concatenate([part.reshape(512, 128) for part in parts], axis=1)
        right = jnp.concatenate([gcoarse[n]] + [gcoarses[k, n] for k in range(3)], axis=0)
        got = dot(left, right).astype(bf16).reshape(4, 4, 32, 256)
        acc_mg[:, :, :, pl.ds(pl.multiple_of(n * 256, 256), 256)] = got
        return carry

    lax.fori_loop(0, 4, grad_merge, 0)
    stream_mg.ring.begin()

    third.arrive()
    for level in range(2):
        gbranch_w[:, level] = third.gather(level, to_window).astype(bf16).reshape(4, 64, 512)
    grads_w = gbranch_w[...].reshape(512, 512)
    gattended[...] = dot_nt(grads_w, w_proj[...]).astype(bf16).reshape(4, 128, 512)
    turned = dot_nt(w_proj[...], grads_w).astype(bf16)
    for w in range(4):
        gattended_t[w] = turned[:, w * 128 : (w + 1) * 128].reshape(4, 128, 128)
    pairs.append(send(gbranch_w, sib_gbranch, asem.at[2], arsem.at[2], where["sibling"]))
    stream_ex.ring.middle()

    def share_window(w):
        return pltpu.make_async_remote_copy(
            src_ref=gqkv.at[:, w],
            dst_ref=sib_gqkv.at[:, w],
            send_sem=asem.at[3 + w],
            recv_sem=arsem.at[3 + w],
            device_id=where["sibling"],
            device_id_type=MESH,
        )

    def attend_back(w, g):
        grads = gattended[w, :, g * 128 : (g + 1) * 128]
        grad_weights = dot(qkv[8 + g, w], head_blocks(gattended_t[w, g]))
        weight = weights[w, g]
        wide = weight.astype(f32)
        shared = wide * grad_weights
        delta = jnp.sum(shared, axis=0, keepdims=True)
        grad_scores = ((shared - wide * delta) * scale).astype(bf16)
        turned = dot(head_blocks(qkv_t[4 + g, w]), under(grad_scores))
        gqkv[g, w] = turned.astype(bf16).T
        gqkv[4 + g, w] = dot(grad_scores, head_stack(qkv[g, w])).astype(bf16)
        gqkv[8 + g, w] = dot(weight, head_stack(grads)).astype(bf16)

    def attend_back_window(w, carry):
        for g in range(4):
            attend_back(w, g)
        share_window(w).start()
        return carry

    lax.fori_loop(0, 2, attend_back_window, 0)
    for made in pairs:
        made.wait_recv()
    left = jnp.concatenate((attended_t[:, core].reshape(256, 512), sib_attended[...].reshape(256, 512)), axis=1)
    right = jnp.concatenate((gbranch_w[...].reshape(512, 512), sib_gbranch[...].reshape(512, 512)), axis=0)
    acc_pj[...] = dot(left, right).astype(bf16).reshape(4, 4, 16, 512)
    stream_pj.ring.begin()
    stream_mg.ring.middle()
    stream_ex.ring.finish()
    stream_ex.spread()
    lax.fori_loop(2, 4, attend_back_window, 0)
    windows = [share_window(w) for w in range(4)]
    for made in windows:
        made.wait_recv()

    def grad_qkv(target, base, n, carry):
        left = jnp.concatenate((normed_t[:, core].reshape(256, 512), sib_normed[...].reshape(256, 512)), axis=1)
        k = 2 * n + base
        own = [gqkv[k + part].reshape(512, 128) for part in range(2)]
        far = [sib_gqkv[k + part].reshape(512, 128) for part in range(2)]
        right = jnp.concatenate((jnp.concatenate(own, axis=1), jnp.concatenate(far, axis=1)), axis=0)
        got = dot(left, right).astype(bf16).reshape(4, 4, 16, 256)
        target[:, :, :, pl.ds(pl.multiple_of(n * 256, 256), 256)] = got
        return carry

    lax.fori_loop(0, 3, functools.partial(grad_qkv, acc_q1, 0), 0)
    stream_q1.ring.begin()
    lax.fori_loop(0, 3, functools.partial(grad_qkv, acc_q2, 6), 0)
    stream_q2.ring.begin()

    def norm_back(half, carry):
        rows = jnp.concatenate([gqkv[n, pl.ds(2 * half, 2)].reshape(256, 128) for n in range(12)], axis=1)
        grad = dot_nt(rows, w_qkv[...]) * gain_attn
        hat = hat_w[pl.ds(2 * half, 2)].reshape(256, 512)
        rstd = rstd_w[pl.ds(2 * half, 2)].reshape(256, 128)[:, 0:1]
        first_mean = jnp.mean(grad, axis=-1, keepdims=True)
        second_mean = jnp.mean(grad * hat, axis=-1, keepdims=True)
        grad = rstd * (grad - first_mean - hat * second_mean)
        grolled[pl.ds(2 * half, 2)] = grad.astype(bf16).reshape(2, 2, 64, 512)
        return carry

    lax.fori_loop(0, 2, norm_back, 0)
    fourth = Exchange(where, grolled, pack_window, exchanges[3])
    fourth.begin()
    stream_mg.ring.finish()
    stream_mg.spread()
    stream_pj.ring.middle()
    stream_q1.ring.middle()
    stream_q2.ring.middle()

    fine_hot = one_hot(fine_code(iota((256, 256), 0)) == patch_code(iota((1, 256), 1)))

    def expand(q, carry):
        rows = jnp.concatenate([act[n] for n in range(4)], axis=1)
        grown = dot(rows, w_expand[:, pl.ds(pl.multiple_of(q * 512, 512), 512)])
        out_patch[q] = (hidden[q].reshape(128, 512).astype(f32) + grown).astype(bf16).reshape(2, 64, 512)
        return carry

    lax.fori_loop(0, 4, expand, 0)
    for level in range(2):
        out_ref[level] = dot(fine_hot, out_patch[:, level].reshape(256, 512)).astype(bf16)

    stream_pj.ring.finish()
    stream_pj.spread()
    stream_q1.ring.finish()
    stream_q1.spread()
    stream_q2.ring.finish()
    stream_q2.spread()
    fourth.arrive()
    for level in range(2):
        back = fourth.gather(level, to_patch).astype(bf16).astype(f32)
        total = (ghidden[:, level].reshape(256, 512) + back).astype(bf16)
        field_ref[level] = dot(fine_hot, total).astype(bf16)

    streams = (stream_ex, stream_mg, stream_pj, stream_q1, stream_q2)
    for stream in streams:
        stream.end()

    for made in sent + pairs + windows:
        made.wait_send()
    for each in (first, second, third, fourth):
        each.drain()
    for stream in streams:
        stream.drain()


def deliver_kernel(*refs):
    sources, targets, held, sems = refs[:6], refs[6:12], refs[12:18], refs[18]
    loads = [pltpu.make_async_copy(a, b, sems.at[0, n]) for n, (a, b) in enumerate(zip(sources, held))]
    stores = [pltpu.make_async_copy(a, b, sems.at[1, n]) for n, (a, b) in enumerate(zip(held, targets))]
    for made in loads:
        made.start()
    for load, store in zip(loads, stores):
        load.wait()
        store.start()
    for made in stores:
        made.wait()


def deliver(results):
    hbm = pl.BlockSpec(memory_space=pl.ANY)
    return pl.pallas_call(
        deliver_kernel,
        out_shape=tuple(jax.ShapeDtypeStruct(r.shape, r.dtype) for r in results),
        in_specs=[hbm] * 6,
        out_specs=(hbm,) * 6,
        scratch_shapes=[pltpu.VMEM(r.shape, r.dtype) for r in results] + [pltpu.SemaphoreType.DMA((2, 6))],
        name="deliver",
    )(*results)


def on_device(
    fine_field,
    cotangent,
    land_sea,
    shifts,
    gain_attn,
    w_qkv,
    w_proj,
    land_bias,
    gain_merge,
    w_merge,
    w_expand,
):
    vmem = pl.BlockSpec(memory_space=pltpu.VMEM)
    smem = pl.BlockSpec(memory_space=pltpu.SMEM)
    hbm = pl.BlockSpec(memory_space=pl.ANY)
    f32, bf16 = jnp.float32, jnp.bfloat16
    cells = (4, 2, 64, 512)
    scratch = [
        pltpu.VMEM((512, 1536), bf16),
        pltpu.VMEM((512, 512), bf16),
        pltpu.VMEM((2048, 1024), bf16),
        pltpu.VMEM((1024, 2048), bf16),
        pltpu.SemaphoreType.DMA((4,)),
        pltpu.VMEM((256, 640), bf16),
        pltpu.VMEM((256, 640), bf16),
        pltpu.VMEM((64, 256), bf16),
        pltpu.VMEM((64, 256), bf16),
        pltpu.VMEM(cells, bf16),
        pltpu.VMEM(cells, bf16),
        pltpu.VMEM(cells, bf16),
        pltpu.VMEM(cells, f32),
        pltpu.VMEM((4, 2, 64, 128), f32),
        pltpu.VMEM((12, 4, 128, 128), bf16),
        pltpu.VMEM((12, 4, 128, 128), bf16),
        pltpu.VMEM((4, 4, 128, 512), bf16),
        pltpu.VMEM(cells, bf16),
        pltpu.VMEM(cells, bf16),
        pltpu.VMEM((128, 2048), f32),
        pltpu.VMEM((128, 128), f32),
        pltpu.VMEM((4, 128, 512), bf16),
        pltpu.VMEM((4, 128, 256), f32),
        pltpu.VMEM((4, 128, 256), bf16),
        pltpu.VMEM((4, 128, 256), bf16),
        pltpu.VMEM(cells, bf16),
        pltpu.VMEM(cells, f32),
        pltpu.VMEM(cells, bf16),
        pltpu.VMEM((3,) + cells, bf16),
        pltpu.VMEM((3, 4, 128, 256), bf16),
        pltpu.VMEM((2, 2, 4, 4, 16, 128), bf16),
        pltpu.VMEM((2, 2, 4, 4, 32, 128), bf16),
        pltpu.VMEM((3, 4, 4, 16, 128), bf16),
        pltpu.VMEM((3, 4, 4, 32, 128), bf16),
        pltpu.SemaphoreType.DMA((12,)),
        pltpu.SemaphoreType.DMA((12,)),
        pltpu.VMEM(cells, bf16),
        pltpu.VMEM((4, 128, 512), bf16),
        pltpu.VMEM((4, 4, 128, 128), bf16),
        pltpu.VMEM((12, 4, 128, 128), bf16),
        pltpu.VMEM(cells, bf16),
        pltpu.VMEM(cells, bf16),
        pltpu.VMEM(cells, bf16),
        pltpu.VMEM((4, 64, 512), bf16),
        pltpu.VMEM((4, 64, 512), bf16),
        pltpu.VMEM(cells, bf16),
        pltpu.VMEM((12, 4, 128, 128), bf16),
        pltpu.SemaphoreType.DMA((7,)),
        pltpu.SemaphoreType.DMA((7,)),
        pltpu.VMEM((4, 4, 16, 2048), bf16),
        pltpu.VMEM((4, 4, 32, 1024), bf16),
        pltpu.VMEM((4, 4, 16, 512), bf16),
        pltpu.VMEM((4, 4, 16, 768), bf16),
        pltpu.VMEM((4, 4, 16, 768), bf16),
    ]
    for _ in range(4):
        scratch += exchange_scratch()
    scratch += stream_scratch(16, 2048, False)
    scratch += stream_scratch(32, 1024, False)
    scratch += stream_scratch(16, 512, True)
    scratch += stream_scratch(16, 768, True)
    scratch += stream_scratch(16, 768, True)
    scratch += [pltpu.VMEM((4, 128, 128), f32)]
    results = pl.pallas_call(
        block_kernel,
        out_shape=(
            jax.ShapeDtypeStruct((2, 256, 512), bf16),
            jax.ShapeDtypeStruct((2, 256, 512), bf16),
            jax.ShapeDtypeStruct((8, 1536), f32),
            jax.ShapeDtypeStruct((8, 512), f32),
            jax.ShapeDtypeStruct((32, 1024), f32),
            jax.ShapeDtypeStruct((16, 2048), f32),
        ),
        in_specs=[smem, smem] + [vmem] * 5 + [hbm] * 4,
        out_specs=(vmem,) * 6,
        scratch_shapes=scratch,
        compiler_params=pltpu.CompilerParams(
            collective_id=0, has_side_effects=True, vmem_limit_bytes=60 * 2**20
        ),
        name="attention_block",
    )(
        shifts,
        land_bias,
        fine_field.reshape(2, 256, 512),
        cotangent.reshape(2, 256, 512),
        land_sea,
        gain_attn.reshape(1, 512),
        gain_merge.reshape(1, 2048),
        w_qkv,
        w_proj,
        w_merge,
        w_expand,
    )
    results = deliver(results)
    output, grad_field = results[0].reshape(2, 8, 32, 512), results[1].reshape(2, 8, 32, 512)
    return (output, grad_field) + tuple(results[2:])


def solution(mesh):
    return jax.shard_map(
        on_device,
        mesh=mesh,
        in_specs=(
            P("rep", "lat", "lon", None),
            P("rep", "lat", "lon", None),
            P(),
            P(),
            P(),
            P(),
            P(),
            P(),
            P(),
            P(),
            P(),
        ),
        out_specs=(
            P("rep", "lat", "lon", None),
            P("rep", "lat", "lon", None),
            P(("rep", "lat", "lon"), None),
            P(("rep", "lat", "lon"), None),
            P(("rep", "lat", "lon"), None),
            P(("rep", "lat", "lon"), None),
        ),
        check_vma=False,
    )
```

time: 101 us -> 90.4 us (0.90); the launches traced: 99.5 us -> 90.2 us
  local copies, waits for them, and re-layouts: 9.64 us -> 0 us
    unnamed x6 -> x0, local copies, waits for them, and re-layouts: 9.64 us -> none
    pallas_call x0 -> x1, Pallas kernels: none -> 2.21 us  [deliver(): pl.pallas_call(deliver_kernel, out_shape=tuple((jax.ShapeDtypeStruct(r.sh...]
    pallas_call x1, Pallas kernels: 89.2 us -> 87.4 us  [on_device(): pl.pallas_call(block_kernel, out_shape=(jax.ShapeDtypeStruct((2, 256, 512...]
where the time goes in v3:
time: 90.4 us; the launch traced here: 90.2 us
  Pallas kernels  89.6 us (99%)
    pallas_call x1, Pallas kernels, on_device(): pl.pallas_call(block_kernel, out_shape=(jax.ShapeDtypeStruct((2, 256, 512...  87.4 us
    pallas_call x1, Pallas kernels, deliver(): pl.pallas_call(deliver_kernel, out_shape=tuple((jax.ShapeDtypeStruct(r.sh...  2.21 us

profile of v3, /device:TPU:1, one launch (start us, length us, event | category | flops | bytes accessed | tf_op | source)
XLA Modules:
  0.0 90.2 jit_solution(12108513760506775285)
XLA Ops:
  0.6 87.4 %attention_block.1 = (bf16[2,256,512]{2,1,0:T(8,128)(2,1)}, bf16[2,256,512]{2,1,0:T(8,128)(2,1)}, f32[8,1536]{1,0:T(8,128)}, f32[8,512]{1,0:T(8,128)}, f32[32,1024]{1,0:T(8,128)}, /*index=5*/f32[16,2048]{1,0:T(8,128)}) custom-call(s32[2]{0:T(128)} %shifts_ref.1, f32[16]{0:T(128)} %bias_ref.1, bf16[2,256,512]{2,1,0:T(8,128)(2,1)} %bitcast.6, ...), custom_call_target="tpu_custom_call" | custom-call | tf_op jit(solution)/shard_map/attention_block/pallas_call | solution.py:921
  88.0 2.2 %deliver.1 = (bf16[2,256,512]{2,1,0:T(8,128)(2,1)}, bf16[2,256,512]{2,1,0:T(8,128)(2,1)}, f32[8,1536]{1,0:T(8,128)}, f32[8,512]{1,0:T(8,128)}, f32[32,1024]{1,0:T(8,128)}, /*index=5*/f32[16,2048]{1,0:T(8,128)}) custom-call(bf16[2,256,512]{2,1,0:T(8,128)(2,1)} %get-tuple-element.18.refs_0_, bf16[2,256,512]{2,1,0:T(8,128)(2,1)} %get-tuple-element.19.refs_1_, ...), custom_call_target="tpu_custom_call" | custom-call | tf_op jit(solution)/shard_map/deliver/pallas_call | solution.py:829

commit v4 on v3

--- a/solution.py
+++ b/solution.py
@@ -88,7 +88,7 @@
         buf, out, red, got, ssem, rsem = scratch
         self.where, self.paired, self.store = where, paired, store
         self.red, self.got, self.ssem, self.rsem = red, got, ssem, rsem
-        self.half = source.shape[3] // 2
+        self.half, self.deep = source.shape[3] // 2, source.shape[2] // 2
         axes = {
             "y": (where["y"], where["up"], where["down"], lambda k: source.at[k]),
             "x": (where["x"], where["east"], where["west"], lambda k: source.at[:, k]),
@@ -101,8 +101,8 @@
     def keep(self, i, first, second):
         if self.paired:
             for z in range(2):
-                rows = slice(z * 8, z * 8 + 8)
-                both = jnp.concatenate((first[rows], second[rows]), axis=0)
+                rows = slice(z * self.deep, (z + 1) * self.deep)
+                both = jnp.concatenate((first[rows], second[rows]), axis=0 if self.deep == 8 else 1)
                 self.red[i, z] = both.astype(jnp.bfloat16)
         else:
             self.red[i] = jnp.concatenate((first, second), axis=1).astype(jnp.bfloat16)
@@ -140,7 +140,7 @@
         total = mine.astype(jnp.float32)
         for n in range(len(self.copies)):
             total += self.got[n].astype(jnp.float32)
-        if self.paired:
+        if self.paired and self.deep == 8:
             total = jnp.concatenate((total[:8], total[8:]), axis=1)
         self.store(total)
 
@@ -152,11 +152,12 @@
 
 def stream_scratch(rows, width, paired):
     half, bf16 = width // 2, jnp.bfloat16
+    block = (16, half) if rows == 16 else (rows // 2, width)
     return [
         pltpu.VMEM((6, 4, rows, half), bf16),
         pltpu.VMEM((2, 4, rows, half), bf16),
-        pltpu.VMEM((4, 2, 16, half) if paired else (4, rows, width), bf16),
-        pltpu.VMEM((7, 16, half) if paired else (3, rows, width), bf16),
+        pltpu.VMEM((4, 2) + block if paired else (4, rows, width), bf16),
+        pltpu.VMEM((7,) + block if paired else (3, rows, width), bf16),
         pltpu.SemaphoreType.DMA((13,)),
         pltpu.SemaphoreType.DMA((13,)),
     ]
@@ -381,9 +382,9 @@
     cots, gcoarses, act_t, merged_t, acts, mergeds, fsem, frsem = take(8)
     gbranch_w, gattended, gattended_t, gqkv, grolled, normed_t, attended_t = take(7)
     sib_normed, sib_attended, sib_gbranch, sib_gqkv, asem, arsem = take(6)
-    acc_ex, acc_mg, acc_pj, acc_q1, acc_q2 = take(5)
+    acc_ex, acc_mg, acc_mh, acc_pj, acc_q1, acc_q2 = take(6)
     exchanges = [take(6) for _ in range(4)]
-    streams_scratch = [take(6) for _ in range(5)]
+    streams_scratch = [take(6) for _ in range(6)]
 
     where = places()
     core, lat, lon = where["core"], where["lat"], where["lon"]
@@ -533,8 +534,6 @@
     second.begin_rim((0, 3))
     lax.fori_loop(2, 4, attend_window, 0)
     pairs.append(send(attended_t.at[:, 1 - core], sib_attended, asem.at[1], arsem.at[1], where["sibling"]))
-    cot_beside.wait_recv()
-    cot_corner = share(2, cots.at[1], cots.at[2], "sibling")
     second.arrive()
     for level in range(2):
         back = second.gather(level, to_patch).reshape(4, 64, 512)
@@ -555,20 +554,18 @@
     for q in range(4):
         merged[q] = scaled[:, q * 512 : (q + 1) * 512]
 
-    def part_rows(target, y, value, deep):
-        value = value.T.reshape(2, 4, 2, deep, 128)
+    def part_rows(target, y, value):
+        value = value.T.reshape(2, 4, 2, 16, 128)
         for c in range(2):
             for z in range(2):
                 target[c, z, y] = value[c, :, z]
 
     for q in range(4):
-        part_rows(merged_t, q, scaled[:, q * 512 : (q + 1) * 512], 32)
+        turned = scaled[:, q * 512 : (q + 1) * 512].T.reshape(2, 256, 128)
+        for c in range(2):
+            merged_t[c, q] = turned[c]
     side, level_z = 1 - core, where["z"]
-    merged_parts = [
-        share(3, merged_t.at[side, level_z], mergeds.at[0], "sibling"),
-        share(4, merged_t.at[core, 1 - level_z], mergeds.at[1], "beside"),
-        share(5, merged_t.at[side, 1 - level_z], mergeds.at[2], "corner"),
-    ]
+    merged_side = share(3, merged_t.at[side], mergeds, "sibling")
 
     loads[2].wait()
     bend = 0.7978845608028654
@@ -580,7 +577,7 @@
         bent = jnp.tanh(bend * (coarse + 0.044715 * (coarse * square)))
         active = (0.5 * coarse * (1.0 + bent)).astype(bf16)
         act[n] = active
-        part_rows(act_t, n, active, 16)
+        part_rows(act_t, n, active)
         inner = bend * (1.0 + 3.0 * 0.044715 * square)
         slope[n] = 0.5 * (1.0 + bent) + 0.5 * coarse * (1.0 - bent * bent) * inner
         return carry
@@ -601,8 +598,9 @@
         return carry
 
     lax.fori_loop(0, 4, back_expand, 0)
-    gcoarse_side = share(9, gcoarse, gcoarses.at[0], "sibling")
-    gcoarse_beside = share(10, gcoarse, gcoarses.at[1], "beside")
+    gcoarse_side = share(9, gcoarse, gcoarses, "sibling")
+    cot_beside.wait_recv()
+    cot_corner = share(2, cots.at[1], cots.at[2], "sibling")
 
     def store_q1(value):
         qkv_out[:, 0:768] = value
@@ -617,30 +615,17 @@
         ex_out[...] = value
 
     def store_mg(value):
-        mg_out[...] = value
-
-    stream_ex = Stream(where, acc_ex, "x", False, streams_scratch[0], store_ex)
-    stream_mg = Stream(where, acc_mg, "y", False, streams_scratch[1], store_mg)
+        mg_out[:, 0:768] = value
+
+    def store_mh(value):
+        mg_out[:, 768:1024] = value
+
+    stream_ex = Stream(where, acc_ex, "y", False, streams_scratch[0], store_ex)
+    stream_mg = Stream(where, acc_mg, "x", True, streams_scratch[1], store_mg)
     stream_pj = Stream(where, acc_pj, "x", True, streams_scratch[2], store_pj)
     stream_q1 = Stream(where, acc_q1, "y", True, streams_scratch[3], store_q1)
     stream_q2 = Stream(where, acc_q2, "x", True, streams_scratch[4], store_q2)
-    for made in act_parts:
-        made.wait_recv()
-    cot_side.wait_recv()
-    cot_corner.wait_recv()
-
-    def grad_expand(q, carry):
-        parts = [act_t[core, level_z]] + [acts[n] for n in range(3)]
-        left = jnp.concatenate([part.reshape(256, 128) for part in parts], axis=1)
-        parts = [c_patch[q]] + [cots[n, q] for n in range(3)]
-        right = jnp.concatenate([part.reshape(128, 512) for part in parts], axis=0)
-        got = dot(left, right).astype(bf16).reshape(4, 4, 16, 512)
-        acc_ex[:, :, :, pl.ds(pl.multiple_of(q * 512, 512), 512)] = got
-        return carry
-
-    lax.fori_loop(0, 4, grad_expand, 0)
-    stream_ex.ring.begin()
-
+    stream_mh = Stream(where, acc_mh, "y", True, streams_scratch[5], store_mh)
     def back_merge(q, carry):
         rows = jnp.concatenate([gcoarse[n] for n in range(4)], axis=1)
         slab = w_merge[pl.ds(pl.multiple_of(q * 512, 512), 512), :]
@@ -667,23 +652,39 @@
     third = Exchange(where, gbranch, pack_patch, exchanges[2])
     third.begin()
 
-    gcoarse_beside.wait_recv()
-    gcoarse_corner = share(11, gcoarses.at[1], gcoarses.at[2], "sibling")
-    for made in merged_parts:
+    merged_side.wait_recv()
+    gcoarse_side.wait_recv()
+
+    def merge_part(n):
+        parts = [merged_t[core].reshape(1024, 128), mergeds[...].reshape(1024, 128)]
+        left = jnp.concatenate(parts, axis=1)
+        right = jnp.concatenate((gcoarse[n], gcoarses[n]), axis=0)
+        return dot(left, right).astype(bf16).reshape(4, 4, 64, 256)
+
+    def grad_merge(n, carry):
+        acc_mg[:, :, :, pl.ds(pl.multiple_of(n * 256, 256), 256)] = merge_part(n)
+        return carry
+
+    lax.fori_loop(0, 3, grad_merge, 0)
+    stream_mg.ring.begin()
+    acc_mh[...] = merge_part(3)
+    stream_mh.ring.begin()
+    for made in act_parts:
         made.wait_recv()
-    gcoarse_side.wait_recv()
-    gcoarse_corner.wait_recv()
-
-    def grad_merge(n, carry):
-        parts = [merged_t[core, level_z]] + [mergeds[k] for k in range(3)]
-        left = jnp.concatenate([part.reshape(512, 128) for part in parts], axis=1)
-        right = jnp.concatenate([gcoarse[n]] + [gcoarses[k, n] for k in range(3)], axis=0)
-        got = dot(left, right).astype(bf16).reshape(4, 4, 32, 256)
-        acc_mg[:, :, :, pl.ds(pl.multiple_of(n * 256, 256), 256)] = got
-        return carry
-
-    lax.fori_loop(0, 4, grad_merge, 0)
-    stream_mg.ring.begin()
+    cot_side.wait_recv()
+    cot_corner.wait_recv()
+
+    def grad_expand(q, carry):
+        parts = [act_t[core, level_z]] + [acts[n] for n in range(3)]
+        left = jnp.concatenate([part.reshape(256, 128) for part in parts], axis=1)
+        parts = [c_patch[q]] + [cots[n, q] for n in range(3)]
+        right = jnp.concatenate([part.reshape(128, 512) for part in parts], axis=0)
+        got = dot(left, right).astype(bf16).reshape(4, 4, 16, 512)
+        acc_ex[:, :, :, pl.ds(pl.multiple_of(q * 512, 512), 512)] = got
+        return carry
+
+    lax.fori_loop(0, 4, grad_expand, 0)
+    stream_ex.ring.begin()
 
     third.arrive()
     for level in range(2):
@@ -694,7 +695,6 @@
     for w in range(4):
         gattended_t[w] = turned[:, w * 128 : (w + 1) * 128].reshape(4, 128, 128)
     pairs.append(send(gbranch_w, sib_gbranch, asem.at[2], arsem.at[2], where["sibling"]))
-    stream_ex.ring.middle()
 
     def share_window(w):
         return pltpu.make_async_remote_copy(
@@ -732,9 +732,9 @@
     right = jnp.concatenate((gbranch_w[...].reshape(512, 512), sib_gbranch[...].reshape(512, 512)), axis=0)
     acc_pj[...] = dot(left, right).astype(bf16).reshape(4, 4, 16, 512)
     stream_pj.ring.begin()
+    stream_ex.ring.middle()
     stream_mg.ring.middle()
-    stream_ex.ring.finish()
-    stream_ex.spread()
+    stream_mh.ring.middle()
     lax.fori_loop(2, 4, attend_back_window, 0)
     windows = [share_window(w) for w in range(4)]
     for made in windows:
@@ -754,6 +754,8 @@
     stream_q1.ring.begin()
     lax.fori_loop(0, 3, functools.partial(grad_qkv, acc_q2, 6), 0)
     stream_q2.ring.begin()
+    stream_ex.ring.finish()
+    stream_ex.spread()
 
     def norm_back(half, carry):
         rows = jnp.concatenate([gqkv[n, pl.ds(2 * half, 2)].reshape(256, 128) for n in range(12)], axis=1)
@@ -769,6 +771,8 @@
     lax.fori_loop(0, 2, norm_back, 0)
     fourth = Exchange(where, grolled, pack_window, exchanges[3])
     fourth.begin()
+    stream_mh.ring.finish()
+    stream_mh.spread()
     stream_mg.ring.finish()
     stream_mg.spread()
     stream_pj.ring.middle()
@@ -799,7 +803,7 @@
         total = (ghidden[:, level].reshape(256, 512) + back).astype(bf16)
         field_ref[level] = dot(fine_hot, total).astype(bf16)
 
-    streams = (stream_ex, stream_mg, stream_pj, stream_q1, stream_q2)
+    streams = (stream_ex, stream_mh, stream_mg, stream_pj, stream_q1, stream_q2)
     for stream in streams:
         stream.end()
 
@@ -884,11 +888,11 @@
         pltpu.VMEM(cells, f32),
         pltpu.VMEM(cells, bf16),
         pltpu.VMEM((3,) + cells, bf16),
-        pltpu.VMEM((3, 4, 128, 256), bf16),
+        pltpu.VMEM((4, 128, 256), bf16),
         pltpu.VMEM((2, 2, 4, 4, 16, 128), bf16),
-        pltpu.VMEM((2, 2, 4, 4, 32, 128), bf16),
+        pltpu.VMEM((2, 4, 256, 128), bf16),
         pltpu.VMEM((3, 4, 4, 16, 128), bf16),
-        pltpu.VMEM((3, 4, 4, 32, 128), bf16),
+        pltpu.VMEM((4, 256, 128), bf16),
         pltpu.SemaphoreType.DMA((12,)),
         pltpu.SemaphoreType.DMA((12,)),
         pltpu.VMEM(cells, bf16),
@@ -905,7 +909,8 @@
         pltpu.SemaphoreType.DMA((7,)),
         pltpu.SemaphoreType.DMA((7,)),
         pltpu.VMEM((4, 4, 16, 2048), bf16),
-        pltpu.VMEM((4, 4, 32, 1024), bf16),
+        pltpu.VMEM((4, 4, 64, 768), bf16),
+        pltpu.VMEM((4, 4, 64, 256), bf16),
         pltpu.VMEM((4, 4, 16, 512), bf16),
         pltpu.VMEM((4, 4, 16, 768), bf16),
         pltpu.VMEM((4, 4, 16, 768), bf16),
@@ -913,10 +918,11 @@
     for _ in range(4):
         scratch += exchange_scratch()
     scratch += stream_scratch(16, 2048, False)
-    scratch += stream_scratch(32, 1024, False)
+    scratch += stream_scratch(64, 768, True)
     scratch += stream_scratch(16, 512, True)
     scratch += stream_scratch(16, 768, True)
     scratch += stream_scratch(16, 768, True)
+    scratch += stream_scratch(64, 256, True)
     scratch += [pltpu.VMEM((4, 128, 128), f32)]
     results = pl.pallas_call(
         block_kernel,

time: 90.4 us -> 83.1 us (0.919)
  Pallas kernels: 89.6 us -> 82.3 us
    pallas_call x1, Pallas kernels: 87.4 us -> 80.1 us  [on_device(): pl.pallas_call(block_kernel, out_shape=(jax.ShapeDtypeStruct((2, 256, 512...]
where the time goes in v4:
time: 83.1 us; the launch traced here: 83 us
  Pallas kernels  82.3 us (99%)
    pallas_call x1, Pallas kernels, on_device(): pl.pallas_call(block_kernel, out_shape=(jax.ShapeDtypeStruct((2, 256, 512...  80.1 us
    pallas_call x1, Pallas kernels, deliver(): pl.pallas_call(deliver_kernel, out_shape=tuple((jax.ShapeDtypeStruct(r.sh...  2.21 us

profile of v4, /device:TPU:1, one launch (start us, length us, event | category | flops | bytes accessed | tf_op | source)
XLA Modules:
  0.0 83.0 jit_solution(6813820267580774914)
XLA Ops:
  0.6 80.1 %attention_block.1 = (bf16[2,256,512]{2,1,0:T(8,128)(2,1)}, bf16[2,256,512]{2,1,0:T(8,128)(2,1)}, f32[8,1536]{1,0:T(8,128)}, f32[8,512]{1,0:T(8,128)}, f32[32,1024]{1,0:T(8,128)}, /*index=5*/f32[16,2048]{1,0:T(8,128)}) custom-call(s32[2]{0:T(128)} %shifts_ref.1, f32[16]{0:T(128)} %bias_ref.1, bf16[2,256,512]{2,1,0:T(8,128)(2,1)} %bitcast.6, ...), custom_call_target="tpu_custom_call" | custom-call | tf_op jit(solution)/shard_map/attention_block/pallas_call | solution.py:927
  80.8 2.2 %deliver.1 = (bf16[2,256,512]{2,1,0:T(8,128)(2,1)}, bf16[2,256,512]{2,1,0:T(8,128)(2,1)}, f32[8,1536]{1,0:T(8,128)}, f32[8,512]{1,0:T(8,128)}, f32[32,1024]{1,0:T(8,128)}, /*index=5*/f32[16,2048]{1,0:T(8,128)}) custom-call(bf16[2,256,512]{2,1,0:T(8,128)(2,1)} %get-tuple-element.18.refs_0_, bf16[2,256,512]{2,1,0:T(8,128)(2,1)} %get-tuple-element.19.refs_1_, ...), custom_call_target="tpu_custom_call" | custom-call | tf_op jit(solution)/shard_map/deliver/pallas_call | solution.py:833

commit v5 on v4

--- a/solution.py
+++ b/solution.py
@@ -350,7 +350,7 @@
     shifts_ref,
     bias_ref,
     fine_ref,
-    cot_ref,
+    cot_hbm,
     land_ref,
     gain_attn_ref,
     gain_merge_ref,
@@ -358,8 +358,8 @@
     w_proj_hbm,
     w_merge_hbm,
     w_expand_hbm,
-    out_ref,
-    field_ref,
+    out_hbm,
+    field_hbm,
     qkv_out,
     proj_out,
     mg_out,
@@ -374,7 +374,9 @@
         return got
 
     f32, bf16 = jnp.float32, jnp.bfloat16
-    w_qkv, w_proj, w_merge, w_expand, wsem = take(5)
+    w_qkv, w_proj, w_merge, w_expand, cot_ref, out_ref, field_ref, wsem = take(8)
+    cot_load = pltpu.make_async_copy(cot_hbm, cot_ref, wsem.at[4])
+    cot_load.start()
     to_window, to_patch, pack_patch, pack_window = take(4)
     x_patch, c_patch, normed_w, hat_w, rstd_w = take(5)
     qkv, qkv_t, weights, branch = take(4)
@@ -414,13 +416,15 @@
 
     fill_pack(pack_patch, patch_code)
     arrange_hot = one_hot(patch_code(iota((256, 256), 0)) == fine_code(iota((1, 256), 1)))
-    for source, target in ((fine_ref, x_patch), (cot_ref, c_patch)):
-        for level in range(2):
-            target[:, level] = dot(arrange_hot, source[level]).astype(bf16).reshape(4, 64, 512)
+    for level in range(2):
+        x_patch[:, level] = dot(arrange_hot, fine_ref[level]).astype(bf16).reshape(4, 64, 512)
     pl.semaphore_wait(barrier, len(around))
 
     first = Exchange(where, x_patch, pack_patch, exchanges[0])
     first.begin()
+    cot_load.wait()
+    for level in range(2):
+        c_patch[:, level] = dot(arrange_hot, cot_ref[level]).astype(bf16).reshape(4, 64, 512)
     sent = []
 
     def share(n, source, target, name):
@@ -754,6 +758,10 @@
     stream_q1.ring.begin()
     lax.fori_loop(0, 3, functools.partial(grad_qkv, acc_q2, 6), 0)
     stream_q2.ring.begin()
+    stream_mg.ring.finish()
+    stream_mg.spread()
+    stream_mh.ring.finish()
+    stream_mh.spread()
     stream_ex.ring.finish()
     stream_ex.spread()
 
@@ -771,14 +779,11 @@
     lax.fori_loop(0, 2, norm_back, 0)
     fourth = Exchange(where, grolled, pack_window, exchanges[3])
     fourth.begin()
-    stream_mh.ring.finish()
-    stream_mh.spread()
-    stream_mg.ring.finish()
-    stream_mg.spread()
     stream_pj.ring.middle()
     stream_q1.ring.middle()
     stream_q2.ring.middle()
 
+    writes = []
     fine_hot = one_hot(fine_code(iota((256, 256), 0)) == patch_code(iota((1, 256), 1)))
 
     def expand(q, carry):
@@ -790,6 +795,8 @@
     lax.fori_loop(0, 4, expand, 0)
     for level in range(2):
         out_ref[level] = dot(fine_hot, out_patch[:, level].reshape(256, 512)).astype(bf16)
+        writes.append(pltpu.make_async_copy(out_ref.at[level], out_hbm.at[level], wsem.at[5 + level]))
+        writes[-1].start()
 
     stream_pj.ring.finish()
     stream_pj.spread()
@@ -802,6 +809,8 @@
         back = fourth.gather(level, to_patch).astype(bf16).astype(f32)
         total = (ghidden[:, level].reshape(256, 512) + back).astype(bf16)
         field_ref[level] = dot(fine_hot, total).astype(bf16)
+        writes.append(pltpu.make_async_copy(field_ref.at[level], field_hbm.at[level], wsem.at[7 + level]))
+        writes[-1].start()
 
     streams = (stream_ex, stream_mh, stream_mg, stream_pj, stream_q1, stream_q2)
     for stream in streams:
@@ -809,6 +818,8 @@
 
     for made in sent + pairs + windows:
         made.wait_send()
+    for made in writes:
+        made.wait()
     for each in (first, second, third, fourth):
         each.drain()
     for stream in streams:
@@ -817,8 +828,16 @@
 
 def deliver_kernel(*refs):
     sources, targets, held, sems = refs[:6], refs[6:12], refs[12:18], refs[18]
-    loads = [pltpu.make_async_copy(a, b, sems.at[0, n]) for n, (a, b) in enumerate(zip(sources, held))]
-    stores = [pltpu.make_async_copy(a, b, sems.at[1, n]) for n, (a, b) in enumerate(zip(held, targets))]
+    pieces = []
+    for array in zip(sources, held, targets):
+        if len(array[0].shape) == 3:
+            for level in range(2):
+                for part in range(2):
+                    pieces.append([ref.at[level, pl.ds(part * 128, 128)] for ref in array])
+        else:
+            pieces.append(array)
+    loads = [pltpu.make_async_copy(a, b, sems.at[0, n]) for n, (a, b, _c) in enumerate(pieces)]
+    stores = [pltpu.make_async_copy(b, c, sems.at[1, n]) for n, (_a, b, c) in enumerate(pieces)]
     for made in loads:
         made.start()
     for load, store in zip(loads, stores):
@@ -835,7 +854,7 @@
         out_shape=tuple(jax.ShapeDtypeStruct(r.shape, r.dtype) for r in results),
         in_specs=[hbm] * 6,
         out_specs=(hbm,) * 6,
-        scratch_shapes=[pltpu.VMEM(r.shape, r.dtype) for r in results] + [pltpu.SemaphoreType.DMA((2, 6))],
+        scratch_shapes=[pltpu.VMEM(r.shape, r.dtype) for r in results] + [pltpu.SemaphoreType.DMA((2, 12))],
         name="deliver",
     )(*results)
 
@@ -863,7 +882,10 @@
         pltpu.VMEM((512, 512), bf16),
         pltpu.VMEM((2048, 1024), bf16),
         pltpu.VMEM((1024, 2048), bf16),
-        pltpu.SemaphoreType.DMA((4,)),
+        pltpu.VMEM((2, 256, 512), bf16),
+        pltpu.VMEM((2, 256, 512), bf16),
+        pltpu.VMEM((2, 256, 512), bf16),
+        pltpu.SemaphoreType.DMA((9,)),
         pltpu.VMEM((256, 640), bf16),
         pltpu.VMEM((256, 640), bf16),
         pltpu.VMEM((64, 256), bf16),
@@ -934,8 +956,8 @@
             jax.ShapeDtypeStruct((32, 1024), f32),
             jax.ShapeDtypeStruct((16, 2048), f32),
         ),
-        in_specs=[smem, smem] + [vmem] * 5 + [hbm] * 4,
-        out_specs=(vmem,) * 6,
+        in_specs=[smem, smem, vmem, hbm] + [vmem] * 3 + [hbm] * 4,
+        out_specs=(hbm, hbm) + (vmem,) * 4,
         scratch_shapes=scratch,
         compiler_params=pltpu.CompilerParams(
             collective_id=0, has_side_effects=True, vmem_limit_bytes=60 * 2**20

time: 83.1 us -> 82.6 us (level)
  no operation moved by 1% of the time
where the time goes in v5:
time: 82.6 us; the launch traced here: 82.5 us
  Pallas kernels  81.8 us (99%)
    pallas_call x1, Pallas kernels, on_device(): pl.pallas_call(block_kernel, out_shape=(jax.ShapeDtypeStruct((2, 256, 512...  79.6 us
    pallas_call x1, Pallas kernels, deliver(): pl.pallas_call(deliver_kernel, out_shape=tuple((jax.ShapeDtypeStruct(r.sh...  2.27 us

profile of v5, /device:TPU:1, one launch (start us, length us, event | category | flops | bytes accessed | tf_op | source)
XLA Modules:
  0.0 82.5 jit_solution(2842617701310165460)
XLA Ops:
  0.6 79.6 %attention_block.1 = (bf16[2,256,512]{2,1,0:T(8,128)(2,1)}, bf16[2,256,512]{2,1,0:T(8,128)(2,1)}, f32[8,1536]{1,0:T(8,128)}, f32[8,512]{1,0:T(8,128)}, f32[32,1024]{1,0:T(8,128)}, /*index=5*/f32[16,2048]{1,0:T(8,128)}) custom-call(s32[2]{0:T(128)} %shifts_ref.1, f32[16]{0:T(128)} %bias_ref.1, bf16[2,256,512]{2,1,0:T(8,128)(2,1)} %bitcast.6, ...), custom_call_target="tpu_custom_call" | custom-call | tf_op jit(solution)/shard_map/attention_block/pallas_call | solution.py:949
  80.2 2.3 %deliver.1 = (bf16[2,256,512]{2,1,0:T(8,128)(2,1)}, bf16[2,256,512]{2,1,0:T(8,128)(2,1)}, f32[8,1536]{1,0:T(8,128)}, f32[8,512]{1,0:T(8,128)}, f32[32,1024]{1,0:T(8,128)}, /*index=5*/f32[16,2048]{1,0:T(8,128)}) custom-call(bf16[2,256,512]{2,1,0:T(8,128)(2,1)} %get-tuple-element.18.refs_0_, bf16[2,256,512]{2,1,0:T(8,128)(2,1)} %get-tuple-element.19.refs_1_, ...), custom_call_target="tpu_custom_call" | custom-call | tf_op jit(solution)/shard_map/deliver/pallas_call | solution.py:852
